TPU v7x, 256 devices: a whole 4x4x8 slice. The times are simulated.
256 devices in a mesh: tm: 16 (over x_lo, z), space: 2 (over core), tensor: 8 (over y, x_hi).
Axes of the slice: x: 4 (x_hi: 2, x_lo: 2; x = x_hi * 2 + x_lo), y: 4, z: 8, core: 2. Of those that a mesh axis runs over, the one named last changes fastest.
Arguments:
- queries: bfloat16 [16, 2, 2, 256, 2048], P('tm', 'space', None, None, 'tensor'), may hold values from -12 to 12
- keys: bfloat16 [16, 2, 2, 256, 2048], P('tm', 'space', None, None, 'tensor'), may hold values from -6 to 6
- values: bfloat16 [16, 2, 2, 256, 2048], P('tm', 'space', None, None, 'tensor'), may hold values from -6 to 6
- attention_output: bfloat16 [16, 2, 2, 256, 2048], P('tm', 'space', None, None, 'tensor'), may hold values from -6 to 6
- row_logsumexp: float32 [16, 2, 2, 16, 256], P('tm', 'space', None, 'tensor'), may hold values from 8 to 10.5
- output_cotangent: bfloat16 [16, 2, 2, 256, 3072], P('tm', 'space'), may hold values from -24 to 24
- output_weight: bfloat16 [2048, 3072], P('tensor'), may hold values from -0.109375 to 0.109375
- adapter_down: bfloat16 [2048, 32], P('tensor'), may hold values from -0.109375 to 0.109375
- adapter_up: bfloat16 [32, 3072], replicated, may hold values from -0.109375 to 0.109375
- head_tile_reach: int32 [16, 3], P('tensor'), may hold values from 0 to 1, as said below
- key_tile_valid: int32 [16, 2, 2], replicated, may hold values from 0 to 1, as said below
Outputs:
- grad_q: bfloat16 [16, 2, 2, 256, 2048], P('tm', 'space', None, None, 'tensor')
- grad_k: bfloat16 [16, 2, 2, 256, 2048], P('tm', 'space', None, None, 'tensor')
- grad_v: bfloat16 [16, 2, 2, 256, 2048], P('tm', 'space', None, None, 'tensor')
- grad_a: float32 [2048, 32], P('tensor')
- up_map_gradient: float32 [32, 3072], P(None, 'tensor')
Inputs may be any that keep to these rules, and one draw needn't show every extreme that they name: `head_tile_reach`: columns are the reach along frames, height and width; in every aligned group of 2 heads some head has reach 1 on all three. `key_tile_valid`: A tile is 0 exactly when it lies in the last p frame tiles or, where q is 1, in the last width tile; p is 1 to 4 and q is 0 or 1, drawn for the whole grid.
All inputs are finite; a program needn't handle non-finite values.
Results may differ from a plain program's by a relative error of at most 0.011.
Values may be sent and summed in bfloat16 or wider, within the bound.
A program may use at most 128 MiB of HBM per device.

v0:
```python
import jax
import jax.numpy as jnp
from jax import lax
from jax.sharding import PartitionSpec as P

adapter_factor = 2.0


def padded(cells, sides, width):
    for axis, dim in sides:
        count = lax.axis_size(axis)
        ends = count - 1
        head = lax.slice_in_dim(cells, 0, width, axis=dim)
        tail = lax.slice_in_dim(cells, cells.shape[dim] - width, cells.shape[dim], axis=dim)
        cells = jnp.concatenate(
            [
                lax.ppermute(tail, axis, [(i, (i + 1) % count) for i in range(ends)]),
                cells,
                lax.ppermute(head, axis, [((i + 1) % count, i) for i in range(ends)]),
            ],
            axis=dim,
        )
    return cells


def width_pairs(step_width, tile_cols):
    if step_width == -1:
        return (slice(1, tile_cols), slice(0, tile_cols - 1))
    if step_width == 1:
        return (slice(0, tile_cols - 1), slice(1, tile_cols))
    return (slice(0, tile_cols), slice(0, tile_cols))


def widen(part, before, after):
    spans = [(0, 0)] * part.ndim
    spans[1] = (before, after)
    return jnp.pad(part, spans)


def body(
    queries,
    keys,
    values,
    attention_output,
    row_logsumexp,
    output_cotangent,
    output_weight,
    adapter_down,
    adapter_up,
    head_tile_reach,
    key_tile_valid,
):
    tile_rows = queries.shape[1]
    tile_cols = queries.shape[2]
    tile_len = queries.shape[3]
    features = queries.shape[4]
    head_count = head_tile_reach.shape[0]
    head_size = features // head_count
    model_width = output_cotangent.shape[4]
    tokens_here = tile_rows * tile_cols * tile_len
    total_tokens = lax.axis_size("tm") * lax.axis_size("space") * tokens_here
    score_scale = head_size ** (-0.5)
    contract_trailing = (((1,), (1,)), ((), ()))
    contract_leading = (((0,), (0,)), ((), ()))
    flattened_gradient = output_cotangent.reshape(tokens_here, model_width)
    mixed_gradient = (
        adapter_factor
        * lax.dot_general(
            flattened_gradient, adapter_up, contract_trailing, preferred_element_type=jnp.float32
        )
    ).astype(jnp.bfloat16)
    frozen_term = lax.dot_general(
        flattened_gradient, output_weight, contract_trailing, preferred_element_type=jnp.float32
    )
    attention_gradient = (
        frozen_term
        + lax.dot_general(
            mixed_gradient, adapter_down, contract_trailing, preferred_element_type=jnp.float32
        )
    ).astype(jnp.bfloat16)
    flattened_output = attention_output.reshape(tokens_here, features)
    adapter_mixed = lax.psum(
        jnp.dot(flattened_output, adapter_down, preferred_element_type=jnp.float32), "tensor"
    )
    mixed_halfway = adapter_mixed.astype(jnp.bfloat16)
    col_width = model_width // lax.axis_size("tensor")
    columns = lax.dynamic_slice_in_dim(
        flattened_gradient, lax.axis_index("tensor") * col_width, col_width, 1
    )
    part_a = lax.dot_general(
        flattened_output, mixed_gradient, contract_leading, preferred_element_type=jnp.float32
    )
    up_map_partial = adapter_factor * lax.dot_general(
        mixed_halfway, columns, contract_leading, preferred_element_type=jnp.float32
    )
    total_a, total_b = lax.psum((part_a, up_map_partial), ("tm", "space"))
    grad_a = total_a / total_tokens
    up_map_gradient = total_b / total_tokens
    shape_five = (tile_rows, tile_cols, tile_len, head_count, head_size)
    dout_rows = attention_gradient.reshape(shape_five)
    query_rows = queries[0].reshape(shape_five)
    row_delta = jnp.sum(
        dout_rows.astype(jnp.float32) * attention_output[0].reshape(shape_five).astype(jnp.float32),
        axis=-1,
    )
    row_delta = jnp.transpose(row_delta, (0, 1, 3, 2))
    lse_rows = row_logsumexp[0]
    padded_valid = jnp.pad(key_tile_valid, ((1, 1), (1, 1), (0, 0)))
    valid_ext = lax.dynamic_slice(
        padded_valid,
        (lax.axis_index("tm"), lax.axis_index("space") * tile_rows, 0),
        (3, tile_rows + 2, tile_cols),
    )
    reach_time = head_tile_reach[:, 0]
    reach_height = head_tile_reach[:, 1]
    reach_width = head_tile_reach[:, 2]
    key_value = jnp.concatenate([keys, values], axis=-1)
    kv_ext = padded(key_value, (("tm", 0), ("space", 1)), 1)
    dq_parts = []
    frame_slabs = []
    for step_time in (-1, 0, 1):
        row_parts = []
        for step_height in (-1, 0, 1):
            kv_rows = kv_ext[1 + step_time, 1 + step_height : 1 + step_height + tile_rows]
            tile_ok = valid_ext[1 + step_time, 1 + step_height : 1 + step_height + tile_rows] == 1
            key_parts = []
            for step_width in (-1, 0, 1):
                query_cols, key_cols = width_pairs(step_width, tile_cols)
                width_count = tile_cols - abs(step_width)
                block_shape = (tile_rows, width_count, tile_len, head_count, head_size)
                kv_block = kv_rows[:, key_cols]
                key_block = kv_block[..., :features].reshape(block_shape)
                value_block = kv_block[..., features:].reshape(block_shape)
                query_block = query_rows[:, query_cols]
                dout_block = dout_rows[:, query_cols]
                heads_ok = (
                    (abs(step_time) <= reach_time)
                    & (abs(step_height) <= reach_height)
                    & (abs(step_width) <= reach_width)
                )
                linked = (
                    tile_ok[:, key_cols][:, :, None, None, None]
                    & heads_ok[None, None, :, None, None]
                )
                scores = (
                    jnp.einsum(
                        "abqhd,abkhd->abhqk",
                        query_block,
                        key_block,
                        preferred_element_type=jnp.float32,
                    )
                    * score_scale
                )
                probs = jnp.where(linked, jnp.exp(scores - lse_rows[:, query_cols][..., None]), 0.0)
                grad_probs = jnp.einsum(
                    "abqhd,abkhd->abhqk",
                    dout_block,
                    value_block,
                    preferred_element_type=jnp.float32,
                )
                dscore = (probs * (grad_probs - row_delta[:, query_cols][..., None])).astype(
                    jnp.bfloat16
                )
                dq_part = jnp.einsum(
                    "abhqk,abkhd->abqhd", dscore, key_block, preferred_element_type=jnp.float32
                )
                dk_part = jnp.einsum(
                    "abhqk,abqhd->abkhd", dscore, query_block, preferred_element_type=jnp.float32
                )
                dv_part = jnp.einsum(
                    "abhqk,abqhd->abkhd",
                    probs.astype(jnp.bfloat16),
                    dout_block,
                    preferred_element_type=jnp.float32,
                )
                joined = jnp.concatenate(
                    [
                        dk_part.reshape(tile_rows, width_count, tile_len, features),
                        dv_part.reshape(tile_rows, width_count, tile_len, features),
                    ],
                    axis=-1,
                )
                if step_width == -1:
                    dq_parts.append(widen(dq_part, 1, 0))
                    key_parts.append(widen(joined, 0, 1))
                elif step_width == 1:
                    dq_parts.append(widen(dq_part, 0, 1))
                    key_parts.append(widen(joined, 1, 0))
                else:
                    dq_parts.append(dq_part)
                    key_parts.append(joined)
            key_total = sum(key_parts[1:], key_parts[0])
            row_parts.append(
                jnp.pad(key_total, ((1 + step_height, 1 - step_height), (0, 0), (0, 0), (0, 0)))
            )
        frame_slabs.append(row_parts[0] + row_parts[1] + row_parts[2])
    grad_ext = jnp.stack(frame_slabs, axis=0)
    dq_total = sum(dq_parts[1:], dq_parts[0])
    frames = padded(grad_ext, (("tm", 0),), 1)
    frame_sum = frames[0] + frames[2] + frames[4]
    rows_ext = padded(frame_sum, (("space", 0),), 1)
    own_rows = rows_ext[2 : tile_rows + 2]
    own_rows = own_rows.at[0].add(rows_ext[0])
    own_rows = own_rows.at[tile_rows - 1].add(rows_ext[tile_rows + 3])
    grad_keys = own_rows[..., :features] * score_scale
    grad_values = own_rows[..., features:]
    grad_q = (
        (dq_total * score_scale)
        .reshape(1, tile_rows, tile_cols, tile_len, features)
        .astype(jnp.bfloat16)
    )
    grad_k = grad_keys[None].astype(jnp.bfloat16)
    grad_v = grad_values[None].astype(jnp.bfloat16)
    return (grad_q, grad_k, grad_v, grad_a, up_map_gradient)


def solution(mesh):
    placed = (
        P("tm", "space", None, None, "tensor"),
        P("tm", "space", None, None, "tensor"),
        P("tm", "space", None, None, "tensor"),
        P("tm", "space", None, None, "tensor"),
        P("tm", "space", None, "tensor", None),
        P("tm", "space", None, None, None),
        P("tensor", None),
        P("tensor", None),
        P(),
        P("tensor", None),
        P(),
    )
    return jax.shard_map(
        body,
        mesh=mesh,
        in_specs=placed,
        out_specs=(
            P("tm", "space", None, None, "tensor"),
            P("tm", "space", None, None, "tensor"),
            P("tm", "space", None, None, "tensor"),
            P("tensor", None),
            P(None, "tensor"),
        ),
        check_vma=False,
    )
```

profile of v0, /device:TPU:15, one launch (start us, length us, event | category | flops | bytes accessed | tf_op | source)
XLA Modules:
  0.0 532.1 jit_solution(14906379326911818950)
XLA Ops:
  7.2 1.9 copy.576
  9.2 1.8 copy.577
  11.0 2.1 fusion.289
  13.1 7.7 %collective-permute-start.1 = (bf16[1,1,2,256,512]{3,4,2,1,0:T(8,128)(2,1)}, bf16[1,1,2,256,512]{3,4,2,1,0:T(8,128)(2,1)}, u32[]{:S(2)}, u32[]{:S(2)}) collective-permute-start(bf16[1,1,2,256,512]{3,4,2,1,0:T(8,128)(2,1)} %get-tuple-element.142), channel_id=1, source_target_pairs={{16,0},{32,16},{48,32},{64,48},{80,64},{96,80},{112,96},{128,112},... | collective-permute-start | bytes 1572872 | tf_op jit(solution)/shard_map/ppermute | solution.py:19
  20.8 1.9 collective-permute-start
  22.8 2.0 fusion.191
  25.7 28.2 %psum.22 = bf16[512,32]{0,1:T(8,128)(2,1)S(1)} all-reduce(f32[512,32]{0,1:T(8,128)S(1)} %fusion.329), channel_id=1, replica_groups=mesh['tm'=16,'space'=2,'tensor'=8] {'tensor'}, use_global_device_ids=true, to_apply=%region_2.0 | all-reduce | flops 16384 | bytes 98304 | tf_op jit(solution)/shard_map/psum | solution.py:82
  54.8 2.4 fusion.319
  78.7 1.8 copy.800
  82.6 3.1 and_reduce_fusion.13
  85.7 2.2 fusion.201
  87.9 5.9 %and_reduce_fusion.1 = (pred[2]{0:T(512)(128)(4,1)}, pred[2]{0:T(512)(128)(4,1)}, pred[2]{0:T(512)(128)(4,1)}, pred[2]{0:T(512)(128)(4,1)}, pred[2]{0:T(512)(128...) fusion(pred[2,1]{1,0:T(4,128)(4,1)S(1)} %get-tuple-element.81, pred[]{:T(512)} %bitcast.162, ...), kind=kLoop, calls=%fused_computation.412 | loop fusion | flops 16 | bytes 26 | tf_op jit(solution)/shard_map/and | solution.py:142
  93.7 3.2 and_reduce_fusion.2
  96.9 163.0 %all-reduce.49.cloned.1.call-done = (f32[256,32]{0,1:T(8,128)}, f32[32,384]{1,0:T(8,128)}) async-done(((f32[256,32]{0,1:T(8,128)}, f32[32,384]{1,0:T(8,128)}), (f32[256,32]{0,1:T(8,128)}, f32[32,384]{1,0:T(8,128)})) %all-reduce.49.cloned.1.call-update) | async-done | bytes 81936 | tf_op jit(solution)/shard_map/psum | solution.py:96
  266.2 1.9 fusion.293
  269.5 1.9 fusion.302
  277.4 2.5 pad_maximum_fusion
  279.9 5.0 collective-permute-start.3
  298.1 2.4 fusion.195
  304.4 1.8 copy.735
  306.2 1.8 copy.734
  310.5 2.3 fusion.207
  353.1 2.0 copy.867
  369.7 1.9 copy.717
  372.6 1.8 copy.716
  377.3 2.3 copy.723
  380.7 2.1 copy.722
  384.9 1.9 fusion.188
  386.8 1.8 copy.837
  388.5 1.9 fusion.282
  390.4 1.8 copy.836
  400.2 1.9 copy.825
  403.0 1.8 copy.824
  407.0 1.9 copy.771
  409.9 1.8 copy.770
  415.5 2.2 copy.831
  418.8 2.0 copy.830
  420.9 1.9 fusion.193
  424.2 2.0 add_bitcast_fusion
  426.2 3.3 collective-permute-start.5
  430.0 2.1 add_bitcast_fusion.1
  432.1 2.5 collective-permute-start.4
  440.2 2.1 copy.776
  451.5 44.6 %collective-permute-done.5 = f32[1,3,2,256,512]{4,3,2,1,0:T(8,128)} collective-permute-done((f32[1,3,2,256,512]{4,3,2,1,0:T(8,128)}, f32[1,3,2,256,512]{4,3,2,1,0:T(8,128)}, u32[]{:S(2)}, u32[]{:S(2)}) %collective-permute-start.5) | collective-permute-done | bytes 3145760 | tf_op jit(solution)/shard_map/ppermute | solution.py:19
  496.1 7.4 %collective-permute-done.4 = f32[1,3,2,256,512]{4,3,2,1,0:T(8,128)} collective-permute-done((f32[1,3,2,256,512]{4,3,2,1,0:T(8,128)}, f32[1,3,2,256,512]{4,3,2,1,0:T(8,128)}, u32[]{:S(2)}, u32[]{:S(2)}) %collective-permute-start.4) | collective-permute-done | bytes 3145760 | tf_op jit(solution)/shard_map/ppermute | solution.py:17
  503.5 4.0 bitcast_add_fusion
  510.7 7.3 %collective-permute-start.7 = (f32[1,2,256,512]{3,2,1,0:T(8,128)}, f32[1,2,256,512]{3,2,1,0:T(8,128)}, u32[]{:S(2)}, u32[]{:S(2)}) collective-permute-start(f32[1,2,256,512]{3,2,1,0:T(8,128)} %get-tuple-element.86), channel_id=1, source_target_pairs={{8,0},{9,1},{10,2},{11,3},{12,4},{13,5},{14,6},{15,7},{24,16},{25,... | collective-permute-start | bytes 3145736 | tf_op jit(solution)/shard_map/ppermute | solution.py:19
  521.1 2.2 fusion.192
  (493 shorter events, 160.1 us)
Async XLA Ops:
  7.2 15.6 %copy-start = (bf16[1,1,2,256,3072]{4,3,2,1,0:T(8,128)(2,1)S(1)}, bf16[1,1,2,256,3072]{4,3,2,1,0:T(8,128)(2,1)}, u32[]{:S(2)}) copy-start(bf16[1,1,2,256,3072]{4,3,2,1,0:T(8,128)(2,1)} %param.20) | copy-start | bytes 9437188
  7.2 252.7 %all-reduce.49.cloned.1.call-start = ((), (), s32[]{:S(2)}) async-start(), calls=%async_computation | async-start | bytes 163840 | tf_op jit(solution)/shard_map/psum | solution.py:96
  11.0 13.8 %copy-start.16 = (bf16[1,1,2,256,256]{4,3,2,1,0:T(8,128)(2,1)S(1)}, bf16[1,1,2,256,256]{4,3,2,1,0:T(8,128)(2,1)}, u32[]{:S(2)}) copy-start(bf16[1,1,2,256,256]{4,3,2,1,0:T(8,128)(2,1)} %param.18) | copy-start | bytes 786436
  11.0 14.6 %copy-start.110 = (bf16[256,32]{0,1:T(8,128)(2,1)S(1)}, bf16[256,32]{0,1:T(8,128)(2,1)}, u32[]{:S(2)}) copy-start(bf16[256,32]{0,1:T(8,128)(2,1)} %param.22) | copy-start | bytes 49156
  13.1 249.6 %collective-permute-start.1 = (bf16[1,1,2,256,512]{3,4,2,1,0:T(8,128)(2,1)}, bf16[1,1,2,256,512]{3,4,2,1,0:T(8,128)(2,1)}, u32[]{:S(2)}, u32[]{:S(2)}) collective-permute-start(bf16[1,1,2,256,512]{3,4,2,1,0:T(8,128)(2,1)} %get-tuple-element.142), channel_id=1, source_target_pairs={{16,0},{32,16},{48,32},{64,48},{80,64},{96,80},{112,96},{128,112},... | collective-permute-start | bytes 1572872 | tf_op jit(solution)/shard_map/ppermute | solution.py:19
  20.8 247.5 %collective-permute-start = (bf16[1,1,2,256,512]{3,4,2,1,0:T(8,128)(2,1)}, bf16[1,1,2,256,512]{3,4,2,1,0:T(8,128)(2,1)}, u32[]{:S(2)}, u32[]{:S(2)}) collective-permute-start(bf16[1,1,2,256,512]{3,4,2,1,0:T(8,128)(2,1)} %get-tuple-element.142), channel_id=1, source_target_pairs={{0,16},{16,32},{32,48},{48,64},{64,80},{80,96},{96,112},{112,128},... | collective-permute-start | bytes 1572872 | tf_op jit(solution)/shard_map/ppermute | solution.py:17
  59.8 9.7 %copy-start.77 = (bf16[1,2,256,256]{2,3,1,0:T(8,128)(2,1)}, bf16[1,2,256,256]{2,3,1,0:T(8,128)(2,1)S(1)}, u32[]{:S(2)}) copy-start(bf16[1,2,256,256]{2,3,1,0:T(8,128)(2,1)S(1)} %get-tuple-element.140) | copy-start | bytes 786436
  61.0 213.7 %copy-start.115 = (f32[2,256]{1,0:T(2,128)}, f32[2,256]{1,0:T(2,128)S(1)}, u32[]{:S(2)}) copy-start(f32[2,256]{1,0:T(2,128)S(1)} %get-tuple-element.154) | copy-start | bytes 6148
  71.6 9.8 %copy-start.81 = (f32[2,256,128]{1,2,0:T(8,128)S(1)}, f32[2,256,128]{1,2,0:T(8,128)}, u32[]{:S(2)}) copy-start(f32[2,256,128]{1,2,0:T(8,128)} %fusion.275) | copy-start | bytes 786436
  81.8 182.7 %copy-start.119 = (f32[2,256]{1,0:T(2,128)S(1)}, f32[2,256]{1,0:T(2,128)}, u32[]{:S(2)}) copy-start(f32[2,256]{1,0:T(2,128)} %copy-done.118) | copy-start | bytes 6148
  277.4 13.9 %copy-start.71 = (f32[2,128,256]{2,1,0:T(8,128)S(1)}, f32[2,128,256]{2,1,0:T(8,128)}, u32[]{:S(2)}) copy-start(f32[2,128,256]{2,1,0:T(8,128)} %fusion.237) | copy-start | bytes 786436
  279.9 12.3 %copy-start.82 = (f32[2,256,128]{1,2,0:T(8,128)S(1)}, f32[2,256,128]{1,2,0:T(8,128)}, u32[]{:S(2)}) copy-start(f32[2,256,128]{1,2,0:T(8,128)} %fusion.281) | copy-start | bytes 786436
  279.9 13.1 %copy-start.73 = (f32[2,128,256]{2,1,0:T(8,128)S(1)}, f32[2,128,256]{2,1,0:T(8,128)}, u32[]{:S(2)}) copy-start(f32[2,128,256]{2,1,0:T(8,128)} %fusion.239) | copy-start | bytes 786436
  279.9 33.9 %collective-permute-start.3 = (bf16[3,1,2,256,512]{3,4,2,1,0:T(8,128)(2,1)}, bf16[3,1,2,256,512]{3,4,2,1,0:T(8,128)(2,1)}, u32[]{:S(2)}, u32[]{:S(2)}) collective-permute-start(bf16[3,1,2,256,512]{3,4,2,1,0:T(8,128)(2,1)} %pad_maximum_fusion), channel_id=1, source_target_pairs={{8,0},{9,1},{10,2},{11,3},{12,4},{13,5},{14,6},{15,7},{24,16},{25,... | collective-permute-start | bytes 4718600 | tf_op jit(solution)/shard_map/ppermute | solution.py:19
  284.8 33.9 %collective-permute-start.2 = (bf16[3,1,2,256,512]{3,4,2,1,0:T(8,128)(2,1)}, bf16[3,1,2,256,512]{3,4,2,1,0:T(8,128)(2,1)}, u32[]{:S(2)}, u32[]{:S(2)}) collective-permute-start(bf16[3,1,2,256,512]{3,4,2,1,0:T(8,128)(2,1)} %pad_maximum_fusion), channel_id=1, source_target_pairs={{0,8},{1,9},{2,10},{3,11},{4,12},{5,13},{6,14},{7,15},{16,24},{17,... | collective-permute-start | bytes 4718600 | tf_op jit(solution)/shard_map/ppermute | solution.py:17
  286.4 8.2 %copy-start.79 = (bf16[1,2,256,256]{2,3,1,0:T(8,128)(2,1)S(1)}, bf16[1,2,256,256]{2,3,1,0:T(8,128)(2,1)}, u32[]{:S(2)}) copy-start(bf16[1,2,256,256]{2,3,1,0:T(8,128)(2,1)} %get-tuple-element.134) | copy-start | bytes 786436
  286.5 8.2 %copy-start.113 = (f32[1,1,2,2,256]{4,3,2,1,0:T(2,128)S(1)}, f32[1,1,2,2,256]{4,3,2,1,0:T(2,128)}, u32[]{:S(2)}) copy-start(f32[1,1,2,2,256]{4,3,2,1,0:T(2,128)} %param.19) | copy-start | bytes 12292
  302.2 8.3 %copy-start.10 = (bf16[2,2,256,256]{2,3,1,0:T(8,128)(2,1)}, bf16[2,2,256,256]{2,3,1,0:T(8,128)(2,1)S(1)}, u32[]{:S(2)}) copy-start(bf16[2,2,256,256]{2,3,1,0:T(8,128)(2,1)S(1)} %fusion.52) | copy-start | bytes 1572868
  302.2 8.3 %copy-start.70 = (f32[1,1,256,256]{3,2,1,0:T(8,128)S(1)}, f32[1,1,256,256]{3,2,1,0:T(8,128)}, u32[]{:S(2)}) copy-start(f32[1,1,256,256]{3,2,1,0:T(8,128)} %copy.746) | copy-start | bytes 786436
  316.0 10.7 %copy-start.101 = (bf16[1,1,256,256]{2,3,1,0:T(8,128)(2,1)}, bf16[1,1,256,256]{2,3,1,0:T(8,128)(2,1)S(1)}, u32[]{:S(2)}) copy-start(bf16[1,1,256,256]{2,3,1,0:T(8,128)(2,1)S(1)} %get-tuple-element.126) | copy-start | bytes 393220
  316.7 27.4 %copy-start.75 = (bf16[1,2,256,256]{2,3,1,0:T(8,128)(2,1)}, bf16[1,2,256,256]{2,3,1,0:T(8,128)(2,1)S(1)}, u32[]{:S(2)}) copy-start(bf16[1,2,256,256]{2,3,1,0:T(8,128)(2,1)S(1)} %get-tuple-element.148) | copy-start | bytes 786436
  364.4 11.3 %copy-start.26 = (bf16[2,256,256]{1,2,0:T(8,128)(2,1)}, bf16[2,256,256]{1,2,0:T(8,128)(2,1)S(1)}, u32[]{:S(2)}) copy-start(bf16[2,256,256]{1,2,0:T(8,128)(2,1)S(1)} %fusion.176) | copy-start | bytes 786436
  377.3 11.3 %copy-start.6 = (bf16[2,2,256,256]{2,3,1,0:T(8,128)(2,1)}, bf16[2,2,256,256]{2,3,1,0:T(8,128)(2,1)S(1)}, u32[]{:S(2)}) copy-start(bf16[2,2,256,256]{2,3,1,0:T(8,128)(2,1)S(1)} %fusion.51) | copy-start | bytes 1572868
  394.8 10.9 %copy-start.33 = (bf16[2,256,256]{1,2,0:T(8,128)(2,1)}, bf16[2,256,256]{1,2,0:T(8,128)(2,1)S(1)}, u32[]{:S(2)}) copy-start(bf16[2,256,256]{1,2,0:T(8,128)(2,1)S(1)} %fusion.182) | copy-start | bytes 786436
  394.9 10.0 %copy-start.117 = (f32[2,256]{1,0:T(2,128)S(1)}, f32[2,256]{1,0:T(2,128)}, u32[]{:S(2)}) copy-start(f32[2,256]{1,0:T(2,128)} %copy-done.115) | copy-start | bytes 6148
  396.8 10.0 %copy-start.105 = (bf16[1,1,256,256]{2,3,1,0:T(8,128)(2,1)S(1)}, bf16[1,1,256,256]{2,3,1,0:T(8,128)(2,1)}, u32[]{:S(2)}) copy-start(bf16[1,1,256,256]{2,3,1,0:T(8,128)(2,1)} %get-tuple-element.196) | copy-start | bytes 393220
  400.2 12.9 %copy-start.35 = (bf16[2,256,256]{1,2,0:T(8,128)(2,1)}, bf16[2,256,256]{1,2,0:T(8,128)(2,1)S(1)}, u32[]{:S(2)}) copy-start(bf16[2,256,256]{1,2,0:T(8,128)(2,1)S(1)} %fusion.189) | copy-start | bytes 786436
  426.2 69.8 %collective-permute-start.5 = (f32[1,3,2,256,512]{4,3,2,1,0:T(8,128)}, f32[1,3,2,256,512]{4,3,2,1,0:T(8,128)}, u32[]{:S(2)}, u32[]{:S(2)}) collective-permute-start(f32[1,3,2,256,512]{4,3,2,1,0:T(8,128)} %add_bitcast_fusion), channel_id=1, source_target_pairs={{16,0},{32,16},{48,32},{64,48},{80,64},{96,80},{112,96},{128,112},... | collective-permute-start | bytes 9437192 | tf_op jit(solution)/shard_map/ppermute | solution.py:19
  432.1 71.4 %collective-permute-start.4 = (f32[1,3,2,256,512]{4,3,2,1,0:T(8,128)}, f32[1,3,2,256,512]{4,3,2,1,0:T(8,128)}, u32[]{:S(2)}, u32[]{:S(2)}) collective-permute-start(f32[1,3,2,256,512]{4,3,2,1,0:T(8,128)} %add_bitcast_fusion.1), channel_id=1, source_target_pairs={{0,16},{16,32},{32,48},{48,64},{64,80},{80,96},{96,112},{112,128},... | collective-permute-start | bytes 9437192 | tf_op jit(solution)/shard_map/ppermute | solution.py:17
  439.0 9.5 %copy-start.8 = (bf16[2,2,256,256]{2,3,1,0:T(8,128)(2,1)}, bf16[2,2,256,256]{2,3,1,0:T(8,128)(2,1)S(1)}, u32[]{:S(2)}) copy-start(bf16[2,2,256,256]{2,3,1,0:T(8,128)(2,1)S(1)} %fusion.48) | copy-start | bytes 1572868
  450.1 53.4 %copy-start.12 = (f32[1,2,256,512]{3,2,1,0:T(8,128)S(1)}, f32[1,2,256,512]{3,2,1,0:T(8,128)}, u32[]{:S(2)}) copy-start(f32[1,2,256,512]{3,2,1,0:T(8,128)} %fusion.201) | copy-start | bytes 3145732
  507.5 11.3 %copy-start.2 = (f32[3,2,256,512]{3,2,1,0:T(8,128)}, f32[3,2,256,512]{3,2,1,0:T(8,128)S(1)}, u32[]{:S(2)}) copy-start(f32[3,2,256,512]{3,2,1,0:T(8,128)S(1)} %bitcast_add_fusion) | copy-start | bytes 9437188
  507.5 10.6 %copy-start.31 = (bf16[2,256,256]{1,2,0:T(8,128)(2,1)S(1)}, bf16[2,256,256]{1,2,0:T(8,128)(2,1)}, u32[]{:S(2)}) copy-start(bf16[2,256,256]{1,2,0:T(8,128)(2,1)} %copy-done.30) | copy-start | bytes 786436
  507.5 10.8 %copy-start.7 = (bf16[2,2,256,256]{2,3,1,0:T(8,128)(2,1)S(1)}, bf16[2,2,256,256]{2,3,1,0:T(8,128)(2,1)}, u32[]{:S(2)}) copy-start(bf16[2,2,256,256]{2,3,1,0:T(8,128)(2,1)} %copy-done.6) | copy-start | bytes 1572868
  507.5 10.8 %copy-start.74 = (bf16[1,2,256,256]{2,3,1,0:T(8,128)(2,1)S(1)}, bf16[1,2,256,256]{2,3,1,0:T(8,128)(2,1)}, u32[]{:S(2)}) copy-start(bf16[1,2,256,256]{2,3,1,0:T(8,128)(2,1)} %get-tuple-element.146) | copy-start | bytes 786436
  507.5 11.0 %copy-start.9 = (bf16[2,2,256,256]{2,3,1,0:T(8,128)(2,1)S(1)}, bf16[2,2,256,256]{2,3,1,0:T(8,128)(2,1)}, u32[]{:S(2)}) copy-start(bf16[2,2,256,256]{2,3,1,0:T(8,128)(2,1)} %copy-done.8) | copy-start | bytes 1572868
  507.5 11.0 %copy-start.85 = (bf16[1,2,256,256]{2,3,1,0:T(8,128)(2,1)S(1)}, bf16[1,2,256,256]{2,3,1,0:T(8,128)(2,1)}, u32[]{:S(2)}) copy-start(bf16[1,2,256,256]{2,3,1,0:T(8,128)(2,1)} %get-tuple-element.197) | copy-start | bytes 786436
  507.5 11.2 %copy-start.5 = (bf16[2,2,256,256]{2,3,1,0:T(8,128)(2,1)S(1)}, bf16[2,2,256,256]{2,3,1,0:T(8,128)(2,1)}, u32[]{:S(2)}) copy-start(bf16[2,2,256,256]{2,3,1,0:T(8,128)(2,1)} %copy-done.4) | copy-start | bytes 1572868
  507.5 11.2 %copy-start.37 = (f32[1,2,256,2,128]{2,4,3,1,0:T(8,128)S(1)}, f32[1,2,256,2,128]{2,4,3,1,0:T(8,128)}, u32[]{:S(2)}) copy-start(f32[1,2,256,2,128]{2,4,3,1,0:T(8,128)} %convolution_bitcast_fusion.4) | copy-start | bytes 1572868
  507.5 11.2 %copy-start.38 = (f32[1,2,256,2,128]{2,4,3,1,0:T(8,128)S(1)}, f32[1,2,256,2,128]{2,4,3,1,0:T(8,128)}, u32[]{:S(2)}) copy-start(f32[1,2,256,2,128]{2,4,3,1,0:T(8,128)} %convolution_bitcast_fusion.7) | copy-start | bytes 1572868
  507.6 11.2 %copy-start.49 = (f32[1,1,256,2,128]{2,4,3,1,0:T(8,128)S(1)}, f32[1,1,256,2,128]{2,4,3,1,0:T(8,128)}, u32[]{:S(2)}) copy-start(f32[1,1,256,2,128]{2,4,3,1,0:T(8,128)} %convolution_bitcast_fusion.17) | copy-start | bytes 786436
  507.6 11.2 %copy-start.50 = (f32[1,1,256,2,128]{2,4,3,1,0:T(8,128)S(1)}, f32[1,1,256,2,128]{2,4,3,1,0:T(8,128)}, u32[]{:S(2)}) copy-start(f32[1,1,256,2,128]{2,4,3,1,0:T(8,128)} %convolution_bitcast_fusion.18) | copy-start | bytes 786436
  507.6 11.2 %copy-start.51 = (f32[1,1,256,2,128]{2,4,3,1,0:T(8,128)S(1)}, f32[1,1,256,2,128]{2,4,3,1,0:T(8,128)}, u32[]{:S(2)}) copy-start(f32[1,1,256,2,128]{2,4,3,1,0:T(8,128)} %convolution_bitcast_fusion.23) | copy-start | bytes 786436
  507.6 11.2 %copy-start.52 = (f32[1,1,256,2,128]{2,4,3,1,0:T(8,128)S(1)}, f32[1,1,256,2,128]{2,4,3,1,0:T(8,128)}, u32[]{:S(2)}) copy-start(f32[1,1,256,2,128]{2,4,3,1,0:T(8,128)} %convolution_bitcast_fusion.24) | copy-start | bytes 786436
  507.6 11.2 %copy-start.53 = (f32[1,1,256,2,128]{2,4,3,1,0:T(8,128)S(1)}, f32[1,1,256,2,128]{2,4,3,1,0:T(8,128)}, u32[]{:S(2)}) copy-start(f32[1,1,256,2,128]{2,4,3,1,0:T(8,128)} %convolution_bitcast_fusion.12) | copy-start | bytes 786436
  507.6 11.2 %copy-start.83 = (bf16[1,2,256,256]{2,3,1,0:T(8,128)(2,1)S(1)}, bf16[1,2,256,256]{2,3,1,0:T(8,128)(2,1)}, u32[]{:S(2)}) copy-start(bf16[1,2,256,256]{2,3,1,0:T(8,128)(2,1)} %get-tuple-element.132) | copy-start | bytes 786436
  509.2 12.0 %collective-permute-start.6 = (f32[1,2,256,512]{3,2,1,0:T(8,128)}, f32[1,2,256,512]{3,2,1,0:T(8,128)}, u32[]{:S(2)}, u32[]{:S(2)}) collective-permute-start(f32[1,2,256,512]{3,2,1,0:T(8,128)} %get-tuple-element.85), channel_id=1, source_target_pairs={{0,8},{1,9},{2,10},{3,11},{4,12},{5,13},{6,14},{7,15},{16,24},{17,... | collective-permute-start | bytes 3145736 | tf_op jit(solution)/shard_map/ppermute | solution.py:17
  510.7 10.4 %collective-permute-start.7 = (f32[1,2,256,512]{3,2,1,0:T(8,128)}, f32[1,2,256,512]{3,2,1,0:T(8,128)}, u32[]{:S(2)}, u32[]{:S(2)}) collective-permute-start(f32[1,2,256,512]{3,2,1,0:T(8,128)} %get-tuple-element.86), channel_id=1, source_target_pairs={{8,0},{9,1},{10,2},{11,3},{12,4},{13,5},{14,6},{15,7},{24,16},{25,... | collective-permute-start | bytes 3145736 | tf_op jit(solution)/shard_map/ppermute | solution.py:19
  (89 other events, 397.7 us)
Sparse Core Ops, SparseCore 0:
  54.9 204.9 all-reduce.48
where the time goes:
time: 543 us; the launch traced here: 532 us
  waiting for transfers between devices  215 us (40%)
  matrix products  99.7 us (18%)
  local copies, waits for them, and re-layouts  96.5 us (18%)
  other arithmetic  44.9 us (8%)
  starting transfers between devices  30.8 us (6%)
  blocking collectives  28.2 us (5%)
  between operations  16.9 us (3%)
    psum x1, waiting for transfers between devices, body(): total_a, total_b = lax.psum((part_a, up_map_partial), ('tm', 'space'))  163 us
    ppermute x4, waiting for transfers between devices, padded(): lax.ppermute(head, axis, [((i + 1) % count, i) for i in range(ends)])  44.6 us
    reshape x27, local copies, waits for them, and re-layouts, body(): dk_part.reshape(tile_rows, width_count, tile_len, features)  31.1 us
    reshape x27, local copies, waits for them, and re-layouts, body(): dv_part.reshape(tile_rows, width_count, tile_len, features)  30.7 us
    psum x1, blocking collectives, body(): lax.psum(jnp.dot(flattened_output, adapter_down, preferred_element_type=j...  28.2 us
    ppermute x4, starting transfers between devices, padded(): lax.ppermute(head, axis, [((i + 1) % count, i) for i in range(ends)])  23.3 us
    dot_general x27, matrix products, body(): jnp.einsum('abqhd,abkhd->abhqk', dout_block, value_block, preferred_eleme...  23.2 us
    dot_general x27, matrix products, body(): jnp.einsum('abqhd,abkhd->abhqk', query_block, key_block, preferred_elemen...  21.9 us
  transfers between devices with their start and end apart: 9, of which 3 were waited for; matrix products, arithmetic and copies ran while one was open for 20% of the time, Pallas kernels for 0%

commit v1 on v0

v1 whole, which is shorter than its diff:
```python
import functools

import jax
import jax.numpy as jnp
from jax import lax
from jax.experimental import pallas as pl
from jax.experimental.pallas import tpu as pltpu
from jax.sharding import PartitionSpec as P

adapter_factor = 2.0
LOG2E = 1.4426950408889634
FAR = 1e30
MESH = pl.DeviceIdType.MESH
NT = (((1,), (1,)), ((), ()))
TN = (((0,), (0,)), ((), ()))
f32 = jnp.float32
bf16 = jnp.bfloat16


def dot(a, b, dims=(((1,), (0,)), ((), ()))):
    return lax.dot_general(a, b, dims, preferred_element_type=f32)


def kernel(
    sizes,
    q_in,
    k_in,
    v_in,
    o_in,
    lse_in,
    cot_in,
    w_in,
    down_in,
    up_in,
    reach,
    valid,
    gq,
    gk,
    gv,
    ga,
    um,
    qb,
    db,
    st,
    kb,
    vb,
    kt_buf,
    o_v,
    lse_v,
    cot_v,
    w_v,
    down_v,
    up_v,
    dsend,
    stsend,
    dmix,
    dk_acc,
    dv_acc,
    rq,
    ret,
    gq_v,
    dkb,
    dvb,
    mx_own,
    mx,
    px_send,
    px,
    mine,
    red,
    rsb,
    agb,
    fin,
    fx,
    lsem,
    q_send,
    q_recv,
    d_send,
    d_recv,
    s_send,
    s_recv,
    kv_send,
    kv_recv,
    r_send,
    r_recv,
    mx_ssem,
    mx_rsem,
    px_sem,
    rs_ssem,
    rs_rsem,
    ag_ssem,
    ag_rsem,
    fx_sem,
    out_send,
    out_recv,
    out_sem,
):
    tile, hd, t_size, g_size, total_tokens, cols = sizes
    t = lax.axis_index("tm")
    h = lax.axis_index("space")
    g = lax.axis_index("tensor")
    other = 1 - h
    left = lax.rem(t + t_size - 1, t_size)
    right = lax.rem(t + 1, t_size)
    scale = hd**-0.5
    mine_lanes = pl.ds(pl.multiple_of(h * hd, hd), hd)
    other_lanes = pl.ds(pl.multiple_of(other * hd, hd), hd)
    sides = (right, left)
    partner = {"space": other}

    def local(src, dst, index):
        return pltpu.make_async_copy(src, dst, lsem.at[index])

    def remote(src, dst, ssem, rsem, where):
        return pltpu.make_async_remote_copy(
            src_ref=src, dst_ref=dst, send_sem=ssem, recv_sem=rsem, device_id=where, device_id_type=MESH
        )

    def rows_of(w):
        return pl.ds(pl.multiple_of(w * tile, tile), tile)

    loads = [
        local(o_in, o_v, 0),
        local(down_in, down_v, 1),
        local(w_in, w_v, 2),
        local(up_in, up_v, 3),
        local(lse_in, lse_v, 4),
        local(q_in.at[:, mine_lanes], qb.at[h], 5),
        local(k_in.at[:, mine_lanes], kb.at[h], 6),
        local(v_in.at[:, mine_lanes], vb.at[h], 7),
    ]
    for copy in loads[:4]:
        copy.start()
    cot_loads = [local(cot_in.at[rows_of(w)], cot_v.at[rows_of(w)], 8 + w) for w in range(2)]
    for copy in cot_loads + loads[4:]:
        copy.start()

    barrier = pltpu.get_barrier_semaphore()
    for step in range(1, t_size):
        pl.semaphore_signal(
            barrier, inc=1, device_id={"tm": lax.rem(t + step, t_size)}, device_id_type=MESH
        )
    for step in range(1, g_size):
        pl.semaphore_signal(
            barrier, inc=1, device_id={"tensor": lax.rem(g + step, g_size)}, device_id_type=MESH
        )
    for where in (partner, {"tm": left, "space": other}, {"tm": right, "space": other}):
        pl.semaphore_signal(barrier, inc=1, device_id=where, device_id_type=MESH)
    pl.semaphore_wait(barrier, t_size + g_size + 1)

    sends = []
    for side in range(2):
        for n in range(2):
            sends.append(
                remote(
                    q_in.at[:, n * hd : (n + 1) * hd],
                    qb.at[2 + 2 * side + h],
                    q_send.at[side * 2 + n],
                    q_recv.at[2 + 2 * side + h],
                    {"tm": sides[side], "space": n},
                )
            )
    q_pair = remote(q_in.at[:, other_lanes], qb.at[h], q_send.at[4], q_recv.at[h], partner)
    k_pair = remote(k_in.at[:, other_lanes], kb.at[h], kv_send.at[0], kv_recv.at[0], partner)
    v_pair = remote(v_in.at[:, other_lanes], vb.at[h], kv_send.at[1], kv_recv.at[1], partner)
    sends += [q_pair, k_pair, v_pair]
    for copy in sends:
        copy.start()

    loads[0].wait()
    loads[1].wait()
    mixed_part = dot(down_v[...], o_v[...], (((0,), (1,)), ((), ())))
    mx_own[...] = mixed_part.astype(bf16)
    mx_sends = []
    for step in range(1, g_size):
        mx_sends.append(
            remote(
                mx_own,
                mx.at[step - 1],
                mx_ssem.at[step - 1],
                mx_rsem.at[step - 1],
                {"tensor": lax.rem(g + step, g_size)},
            )
        )
    for copy in mx_sends:
        copy.start()

    loads[2].wait()
    loads[3].wait()
    loads[4].wait()

    def grad_sends(w):
        copies = []
        rows = rows_of(w)
        for side in range(2):
            for n in range(2):
                slot = 2 + 2 * side + h
                where = {"tm": sides[side], "space": n}
                index = side * 2 + n
                copies.append(
                    remote(
                        stsend.at[n, w], st.at[slot, w], s_send.at[w, index], s_recv.at[slot, w], where
                    )
                )
                copies.append(
                    remote(
                        dsend.at[n, rows],
                        db.at[slot, rows],
                        d_send.at[w, index],
                        d_recv.at[slot, w],
                        where,
                    )
                )
        copies.append(
            remote(stsend.at[other, w], st.at[h, w], s_send.at[w, 4], s_recv.at[h, w], partner)
        )
        copies.append(
            remote(dsend.at[other, rows], db.at[h, rows], d_send.at[w, 4], d_recv.at[h, w], partner)
        )
        return copies

    def project(w, carry):
        rows = rows_of(w)
        pltpu.make_async_copy(cot_in.at[rows], cot_v.at[rows], lsem.at[8 + w]).wait()
        cot = cot_v[rows, :]
        down_grad = (adapter_factor * dot(cot, up_v[...], NT)).astype(bf16)
        dmix[rows, :] = down_grad
        grad = (dot(cot, w_v[...], NT) + dot(down_grad, down_v[...], NT)).astype(bf16)
        product = (grad.astype(f32) * o_v[rows, :].astype(f32)).T
        for n in range(2):
            delta = jnp.sum(product[n * hd : (n + 1) * hd, :], axis=0, keepdims=True)
            stsend[n, w, 0:1, :] = lse_v[w, n : n + 1, :] * LOG2E
            stsend[n, w, 1:2, :] = delta
            dsend[n, rows, :] = grad[:, n * hd : (n + 1) * hd]
        db[h, rows, :] = dsend[h, rows, :]
        st[h, w] = stsend[h, w]
        for copy in grad_sends(w):
            copy.start()
        return carry

    lax.fori_loop(0, 2, project, 0)

    for copy in mx_sends:
        copy.wait_recv()
    mixed = mx_own[...].astype(f32)
    for step in range(1, g_size):
        mixed += mx[step - 1].astype(f32)
    columns = pl.ds(pl.multiple_of(g * cols, 128), cols)
    up_part = dot(mixed.astype(bf16), cot_v[:, columns]) * (adapter_factor / total_tokens)
    a_part = dot(dmix[...], o_v[...], TN) * (1.0 / total_tokens)
    width = mine.shape[1]
    if width > a_part.shape[1]:
        a_part = jnp.concatenate(
            [a_part, jnp.zeros((a_part.shape[0], width - a_part.shape[1]), f32)], axis=1
        )
    first = h == 0
    mine[...] = jnp.where(first, up_part, a_part)
    px_send[...] = jnp.where(first, a_part, up_part)
    px_copy = remote(px_send, px, px_sem.at[0], px_sem.at[1], partner)
    px_copy.start()

    for copy in loads[5:]:
        copy.wait()
    k_pair.wait_recv()
    v_pair.wait_recv()
    dk_acc[...] = jnp.zeros_like(dk_acc)
    dv_acc[...] = jnp.zeros_like(dv_acc)
    for row in range(2):
        kt_buf[:, row * 2 * tile : (row + 1) * 2 * tile] = kb[row].T

    reach_t = reach[h, 0]
    reach_h = reach[h, 1]
    reach_w = reach[h, 2]

    share = red.shape[1]

    def reduce_sends():
        copies = []
        for step in range(1, t_size):
            peer = lax.rem(t + step, t_size)
            copies.append(
                remote(
                    red.at[peer],
                    rsb.at[step - 1],
                    rs_ssem.at[step - 1],
                    rs_rsem.at[step - 1],
                    {"tm": peer},
                )
            )
        return copies

    def gather_sends():
        copies = []
        for step in range(1, t_size):
            copies.append(
                remote(
                    agb.at[t],
                    agb.at[t],
                    ag_ssem.at[step - 1],
                    ag_rsem.at[step - 1],
                    {"tm": lax.rem(t + step, t_size)},
                )
            )
        return copies

    def locate(u):
        v = u - 4
        near = u < 4
        hq = jnp.where(near, lax.rem(h + u // 2, 2), lax.rem(v // 2 + 2, 2))
        w = jnp.where(near, lax.rem(u, 2), v // 4)
        f = jnp.where(near, 0, 1 + lax.rem(v + 4, 2))
        return near, hq, w, f

    def back(u):
        _, hq, w, f = locate(u)
        rows = rows_of(w)
        where = {"tm": jnp.where(f == 1, left, right), "space": hq}
        slot = jnp.where(f == 1, 1, 0)
        return remote(
            rq.at[u], ret.at[slot, h, rows], r_send.at[u], r_recv.at[slot * 2 + h, w], where
        )

    def back_pair(u):
        _, hq, w, f = locate(u)
        return remote(
            rq.at[u], ret.at[2, h, rows_of(w)], r_send.at[u], r_recv.at[4 + h, w], partner
        )

    def step(u, carry):
        near, hq, w, f = locate(u)
        slot = f * 2 + hq
        rows = rows_of(w)

        @pl.when(u >= 2)
        def _():
            remote(st.at[slot, w], st.at[slot, w], s_send.at[0, 0], s_recv.at[slot, w], partner).wait_recv()
            remote(
                db.at[slot, rows], db.at[slot, rows], d_send.at[0, 0], d_recv.at[slot, w], partner
            ).wait_recv()

        @pl.when((u >= 2) & (w == 0))
        def _():
            remote(qb.at[slot], qb.at[slot], q_send.at[0], q_recv.at[slot], partner).wait_recv()

        @pl.when(u == 4)
        def _():
            px_copy.wait_recv()
            chip = mine[...] + px[...]
            for p in range(t_size):
                red[p] = chip[p * share : (p + 1) * share, :]
            for copy in reduce_sends():
                copy.start()

        @pl.when(u == 8)
        def _():
            for copy in reduce_sends():
                copy.wait_recv()
            total = red[t]
            for index in range(t_size - 1):
                total += rsb[index]
            agb[t] = total
            for copy in gather_sends():
                copy.start()

        q = qb[slot, rows, :]
        d = db[slot, rows, :]
        lse = st[slot, w, 0:1, :]
        delta = st[slot, w, 1:2, :]
        frame = t + jnp.where(f == 0, 0, jnp.where(f == 1, -1, 1))
        frame_ok = (frame >= 0) & (frame < t_size) & (jnp.where(f == 0, 0, 1) <= reach_t)
        dq = None
        for kt in range(4):
            hk, wk = kt // 2, kt % 2
            linked = (
                frame_ok
                & (jnp.abs(hq - hk) <= reach_h)
                & (jnp.abs(w - wk) <= reach_w)
                & (valid[t, hk, wk] == 1)
            )
            shift = lse + jnp.where(linked, 0.0, FAR)
            k = kb[hk, wk * tile : (wk + 1) * tile, :]
            v = vb[hk, wk * tile : (wk + 1) * tile, :]
            probs = jnp.exp2(dot(k, q, NT) * (scale * LOG2E) - shift)
            dprobs = dot(v, d, NT)
            dscore = (probs * (dprobs - delta)).astype(bf16)
            span = slice(kt * tile, (kt + 1) * tile)
            dv_acc[span, :] += dot(probs.astype(bf16), d)
            dk_acc[span, :] += dot(dscore, q)
            part = dot(kt_buf[:, span], dscore)
            dq = part if dq is None else dq + part
        rq[u] = (dq * scale).T.astype(bf16)

        @pl.when(u >= 4)
        def _():
            back(u).start()

        @pl.when((u >= 2) & (u < 4))
        def _():
            back_pair(u).start()

        @pl.when(u < 2)
        def _():
            ret[2, h, rows, :] = rq[u]

        return carry

    lax.fori_loop(0, 12, step, 0)

    for row in range(2):
        dkb[row] = (dk_acc[row * 2 * tile : (row + 1) * 2 * tile, :] * scale).astype(bf16)
        dvb[row] = dv_acc[row * 2 * tile : (row + 1) * 2 * tile, :].astype(bf16)
    pair_out = [
        remote(dkb.at[other], gk.at[:, mine_lanes], out_send.at[0], out_recv.at[0], partner),
        remote(dvb.at[other], gv.at[:, mine_lanes], out_send.at[1], out_recv.at[1], partner),
    ]
    own_out = [
        pltpu.make_async_copy(dkb.at[h], gk.at[:, mine_lanes], out_sem.at[0]),
        pltpu.make_async_copy(dvb.at[h], gv.at[:, mine_lanes], out_sem.at[1]),
    ]
    for copy in pair_out + own_out:
        copy.start()

    gathers = gather_sends()
    for copy in gathers:
        copy.wait_recv()
    for p in range(t_size):
        fin[p * share : (p + 1) * share, :] = agb[p]
    fx_copy = remote(fin, fx, fx_sem.at[0], fx_sem.at[1], partner)
    fx_copy.start()

    for w in range(2):
        rows = rows_of(w)
        for slot in range(4):
            remote(
                ret.at[slot // 2, slot % 2, rows],
                ret.at[slot // 2, slot % 2, rows],
                r_send.at[0],
                r_recv.at[slot, w],
                partner,
            ).wait_recv()
        remote(
            ret.at[2, other, rows], ret.at[2, other, rows], r_send.at[0], r_recv.at[4 + other, w], partner
        ).wait_recv()
        for n in range(2):
            total = (
                ret[0, n, rows, :].astype(f32)
                + ret[1, n, rows, :].astype(f32)
                + ret[2, n, rows, :].astype(f32)
            )
            gq_v[rows, n * hd : (n + 1) * hd] = total.astype(bf16)
    gq_copy = pltpu.make_async_copy(gq_v, gq, out_sem.at[2])
    gq_copy.start()

    fx_copy.wait_recv()
    um[...] = jnp.where(first, fin[...], fx[...])[:, :cols]
    ga[...] = jnp.where(first, fx[...], fin[...])[:, : ga.shape[0]].T

    for copy in sends + mx_sends + [px_copy, fx_copy] + pair_out + gathers + reduce_sends():
        copy.wait_send()
    for w in range(2):
        for copy in grad_sends(w):
            copy.wait_send()

    def drain(u, carry):
        back(u).wait_send()
        return carry

    lax.fori_loop(4, 12, drain, 0)
    for u in (2, 3):
        back_pair(u).wait_send()
    for copy in pair_out:
        copy.wait_recv()
    for copy in own_out + [gq_copy]:
        copy.wait()


def body(
    queries,
    keys,
    values,
    attention_output,
    row_logsumexp,
    output_cotangent,
    output_weight,
    adapter_down,
    adapter_up,
    head_tile_reach,
    key_tile_valid,
):
    tile = queries.shape[3]
    features = queries.shape[4]
    tokens = queries.shape[2] * tile
    heads = head_tile_reach.shape[0]
    hd = features // heads
    rank = adapter_down.shape[1]
    model = output_cotangent.shape[4]
    t_size = lax.axis_size("tm")
    g_size = lax.axis_size("tensor")
    total_tokens = t_size * lax.axis_size("space") * tokens
    cols = model // g_size
    width = max(cols, features)
    share = rank // t_size
    sizes = (tile, hd, t_size, g_size, total_tokens, cols)

    def flat(array):
        return array.reshape(tokens, array.shape[-1])

    anywhere = pl.BlockSpec(memory_space=pl.ANY)
    vmem = pl.BlockSpec(memory_space=pltpu.VMEM)
    smem = pl.BlockSpec(memory_space=pltpu.SMEM)
    dma = pltpu.SemaphoreType.DMA
    grads = jax.ShapeDtypeStruct((tokens, features), bf16)
    scratch = [
        pltpu.VMEM((6, tokens, hd), bf16),
        pltpu.VMEM((6, tokens, hd), bf16),
        pltpu.VMEM((6, 2, 8, tile), f32),
        pltpu.VMEM((2, tokens, hd), bf16),
        pltpu.VMEM((2, tokens, hd), bf16),
        pltpu.VMEM((hd, 2 * tokens), bf16),
        pltpu.VMEM((tokens, features), bf16),
        pltpu.VMEM((2, heads, tile), f32),
        pltpu.VMEM((tokens, model), bf16),
        pltpu.VMEM((features, model), bf16),
        pltpu.VMEM((features, rank), bf16),
        pltpu.VMEM((rank, model), bf16),
        pltpu.VMEM((2, tokens, hd), bf16),
        pltpu.VMEM((2, 2, 8, tile), f32),
        pltpu.VMEM((tokens, rank), bf16),
        pltpu.VMEM((2 * tokens, hd), f32),
        pltpu.VMEM((2 * tokens, hd), f32),
        pltpu.VMEM((12, tile, hd), bf16),
        pltpu.VMEM((3, 2, tokens, hd), bf16),
        pltpu.VMEM((tokens, features), bf16),
        pltpu.VMEM((2, tokens, hd), bf16),
        pltpu.VMEM((2, tokens, hd), bf16),
        pltpu.VMEM((rank, tokens), bf16),
        pltpu.VMEM((g_size - 1, rank, tokens), bf16),
        pltpu.VMEM((rank, width), f32),
        pltpu.VMEM((rank, width), f32),
        pltpu.VMEM((rank, width), f32),
        pltpu.VMEM((t_size, share, width), f32),
        pltpu.VMEM((t_size - 1, share, width), f32),
        pltpu.VMEM((t_size, share, width), f32),
        pltpu.VMEM((rank, width), f32),
        pltpu.VMEM((rank, width), f32),
        dma((10,)),
        dma((5,)),
        dma((6,)),
        dma((2, 5)),
        dma((6, 2)),
        dma((2, 5)),
        dma((6, 2)),
        dma((2,)),
        dma((2,)),
        dma((12,)),
        dma((6, 2)),
        dma((g_size - 1,)),
        dma((g_size - 1,)),
        dma((2,)),
        dma((t_size - 1,)),
        dma((t_size - 1,)),
        dma((t_size - 1,)),
        dma((t_size - 1,)),
        dma((2,)),
        dma((2,)),
        dma((2,)),
        dma((3,)),
    ]
    grad_q, grad_k, grad_v, grad_a, up_map_gradient = pl.pallas_call(
        functools.partial(kernel, sizes),
        out_shape=(
            grads,
            grads,
            grads,
            jax.ShapeDtypeStruct((features, rank), f32),
            jax.ShapeDtypeStruct((rank, cols), f32),
        ),
        in_specs=[anywhere] * 9 + [smem] * 2,
        out_specs=(anywhere, anywhere, anywhere, vmem, vmem),
        scratch_shapes=scratch,
        compiler_params=pltpu.CompilerParams(
            collective_id=0, has_side_effects=True, vmem_limit_bytes=48 * 1024 * 1024
        ),
    )(
        flat(queries),
        flat(keys),
        flat(values),
        flat(attention_output),
        row_logsumexp.reshape(row_logsumexp.shape[2:]),
        flat(output_cotangent),
        output_weight,
        adapter_down,
        adapter_up,
        head_tile_reach,
        key_tile_valid,
    )
    return (
        grad_q.reshape(queries.shape),
        grad_k.reshape(queries.shape),
        grad_v.reshape(queries.shape),
        grad_a,
        up_map_gradient,
    )


def solution(mesh):
    placed = (
        P("tm", "space", None, None, "tensor"),
        P("tm", "space", None, None, "tensor"),
        P("tm", "space", None, None, "tensor"),
        P("tm", "space", None, None, "tensor"),
        P("tm", "space", None, "tensor", None),
        P("tm", "space", None, None, None),
        P("tensor", None),
        P("tensor", None),
        P(),
        P("tensor", None),
        P(),
    )
    return jax.shard_map(
        body,
        mesh=mesh,
        in_specs=placed,
        out_specs=(
            P("tm", "space", None, None, "tensor"),
            P("tm", "space", None, None, "tensor"),
            P("tm", "space", None, None, "tensor"),
            P("tensor", None),
            P(None, "tensor"),
        ),
        check_vma=False,
    )
```

time: 543 us -> 63.6 us (0.12)
  the two profiles are of different devices: /device:TPU:15 before, /device:TPU:1 now
where the time goes in v1:
time: 63.6 us; the launch traced here: 63.3 us
  Pallas kernels  50.1 us (79%)
  local copies, waits for them, and re-layouts  12.5 us (20%)
  between operations  0.66 us (1%)
    pallas_call x1, Pallas kernels, body(): pl.pallas_call(functools.partial(kernel, sizes), out_shape=(grads, grads,...  50.1 us
    unnamed x23, local copies, waits for them, and re-layouts  12.5 us

profile of v1, /device:TPU:1, one launch (start us, length us, event | category | flops | bytes accessed | tf_op | source)
XLA Modules:
  0.0 63.3 jit_solution(2931099979479374214)
XLA Ops:
  0.6 0.8 %copy.17.valid = s32[16,2,2]{2,1,0:T(2,128)S(1)} copy(s32[16,2,2]{0,2,1:T(2,128)} %param.21) | data formatting | bytes 512 | tf_op args[10]
  1.4 0.8 %copy.16.down_in = bf16[256,32]{1,0:T(8,128)(2,1)S(1)} copy(bf16[256,32]{0,1:T(8,128)(2,1)} %param.18) | data formatting | bytes 32768 | tf_op args[7]
  2.2 0.0 copy-start
  2.2 1.4 %copy-done = bf16[256,3072]{1,0:T(8,128)(2,1)S(1)} copy-done((bf16[256,3072]{1,0:T(8,128)(2,1)S(1)}, bf16[256,3072]{1,0:T(8,128)(2,1)}, u32[]{:S(2)}) %copy-start) | copy-done | bytes 1572888
  3.6 0.0 copy-start.1
  3.7 0.9 %copy-done.1 = bf16[1,1,2,256,256]{4,3,2,1,0:T(8,128)(2,1)S(1)} copy-done((bf16[1,1,2,256,256]{4,3,2,1,0:T(8,128)(2,1)S(1)}, bf16[1,1,2,256,256]{4,3,2,1,0:T(8,128)(2,1)}, u32[]{:S(2)}) %copy-start.1) | copy-done | bytes 262168
  4.6 0.0 copy-start.2
  4.6 0.9 %copy-done.2 = bf16[1,1,2,256,256]{4,3,2,1,0:T(8,128)(2,1)S(1)} copy-done((bf16[1,1,2,256,256]{4,3,2,1,0:T(8,128)(2,1)S(1)}, bf16[1,1,2,256,256]{4,3,2,1,0:T(8,128)(2,1)}, u32[]{:S(2)}) %copy-start.2) | copy-done | bytes 262168
  5.5 0.0 copy-start.3
  5.6 0.9 %copy-done.3 = bf16[1,1,2,256,256]{4,3,2,1,0:T(8,128)(2,1)S(1)} copy-done((bf16[1,1,2,256,256]{4,3,2,1,0:T(8,128)(2,1)S(1)}, bf16[1,1,2,256,256]{4,3,2,1,0:T(8,128)(2,1)}, u32[]{:S(2)}) %copy-start.3) | copy-done | bytes 262168
  6.5 0.0 copy-start.4
  6.5 0.9 %copy-done.4 = bf16[1,1,2,256,256]{4,3,2,1,0:T(8,128)(2,1)S(1)} copy-done((bf16[1,1,2,256,256]{4,3,2,1,0:T(8,128)(2,1)S(1)}, bf16[1,1,2,256,256]{4,3,2,1,0:T(8,128)(2,1)}, u32[]{:S(2)}) %copy-start.4) | copy-done | bytes 262168
  7.5 0.0 copy-start.5
  7.5 0.9 %copy-done.5 = bf16[32,3072]{1,0:T(8,128)(2,1)S(1)} copy-done((bf16[32,3072]{1,0:T(8,128)(2,1)S(1)}, bf16[32,3072]{1,0:T(8,128)(2,1)}, u32[]{:S(2)}) %copy-start.5) | copy-done | bytes 196632
  8.4 0.0 copy-start.6
  8.4 0.7 %copy-done.6 = f32[1,1,2,2,256]{4,3,2,1,0:T(2,128)S(1)} copy-done((f32[1,1,2,2,256]{4,3,2,1,0:T(2,128)S(1)}, f32[1,1,2,2,256]{4,3,2,1,0:T(2,128)}, u32[]{:S(2)}) %copy-start.6) | copy-done | bytes 4120
  9.1 0.0 copy-start.7
  9.1 0.7 %copy-done.7 = s32[2,3]{1,0:T(2,128)S(1)} copy-done((s32[2,3]{1,0:T(2,128)S(1)}, s32[2,3]{1,0:T(2,128)}, u32[]{:S(2)}) %copy-start.7) | copy-done | bytes 48
  9.7 50.1 %shard_map.146 = (bf16[512,256]{1,0:T(8,128)(2,1)S(1)}, bf16[512,256]{1,0:T(8,128)(2,1)S(1)}, bf16[512,256]{1,0:T(8,128)(2,1)S(1)}, f32[256,32]{1,0:T(8,128)S(1)}, f32[32,384]{1,0:T(8,128)S(1)}) custom-call(bf16[512,256]{1,0:T(8,128)(2,1)S(1)} %bitcast.9, bf16[512,256]{1,0:T(8,128)(2,1)S(1)} %bitcast.10, bf16[512,256]{1,0:T(8,128)(2,1)S(1)} %bitcast.11, ...), custom_call_target="tpu_custom_call" | custom-call | tf_op jit(solution)/shard_map/pallas_call | solution.py:568
  59.8 0.7 %copy.18 = f32[256,32]{0,1:T(8,128)} copy(f32[256,32]{1,0:T(8,128)S(1)} %get-tuple-element.18) | data formatting | bytes 65536
  60.5 0.7 %copy.23 = bf16[1,1,2,256,256]{4,3,2,1,0:T(8,128)(2,1)} copy(bf16[1,1,2,256,256]{4,3,2,1,0:T(8,128)(2,1)S(1)} %bitcast.15) | data formatting | bytes 524288
  61.2 0.7 %copy.24 = bf16[1,1,2,256,256]{4,3,2,1,0:T(8,128)(2,1)} copy(bf16[1,1,2,256,256]{4,3,2,1,0:T(8,128)(2,1)S(1)} %bitcast.14) | data formatting | bytes 524288
  61.9 0.7 %copy.25 = bf16[1,1,2,256,256]{4,3,2,1,0:T(8,128)(2,1)} copy(bf16[1,1,2,256,256]{4,3,2,1,0:T(8,128)(2,1)S(1)} %bitcast.13) | data formatting | bytes 524288
  62.6 0.6 copy.26
Async XLA Ops:
  2.2 1.4 %copy-start = (bf16[256,3072]{1,0:T(8,128)(2,1)S(1)}, bf16[256,3072]{1,0:T(8,128)(2,1)}, u32[]{:S(2)}) copy-start(bf16[256,3072]{1,0:T(8,128)(2,1)} %w_in.1) | copy-start | bytes 4718596
  3.6 0.9 %copy-start.1 = (bf16[1,1,2,256,256]{4,3,2,1,0:T(8,128)(2,1)S(1)}, bf16[1,1,2,256,256]{4,3,2,1,0:T(8,128)(2,1)}, u32[]{:S(2)}) copy-start(bf16[1,1,2,256,256]{4,3,2,1,0:T(8,128)(2,1)} %param.11) | copy-start | bytes 786436
  4.6 0.9 %copy-start.2 = (bf16[1,1,2,256,256]{4,3,2,1,0:T(8,128)(2,1)S(1)}, bf16[1,1,2,256,256]{4,3,2,1,0:T(8,128)(2,1)}, u32[]{:S(2)}) copy-start(bf16[1,1,2,256,256]{4,3,2,1,0:T(8,128)(2,1)} %param.12) | copy-start | bytes 786436
  5.5 0.9 %copy-start.3 = (bf16[1,1,2,256,256]{4,3,2,1,0:T(8,128)(2,1)S(1)}, bf16[1,1,2,256,256]{4,3,2,1,0:T(8,128)(2,1)}, u32[]{:S(2)}) copy-start(bf16[1,1,2,256,256]{4,3,2,1,0:T(8,128)(2,1)} %param.13) | copy-start | bytes 786436
  6.5 0.9 %copy-start.4 = (bf16[1,1,2,256,256]{4,3,2,1,0:T(8,128)(2,1)S(1)}, bf16[1,1,2,256,256]{4,3,2,1,0:T(8,128)(2,1)}, u32[]{:S(2)}) copy-start(bf16[1,1,2,256,256]{4,3,2,1,0:T(8,128)(2,1)} %param.14) | copy-start | bytes 786436
  7.5 0.9 %copy-start.5 = (bf16[32,3072]{1,0:T(8,128)(2,1)S(1)}, bf16[32,3072]{1,0:T(8,128)(2,1)}, u32[]{:S(2)}) copy-start(bf16[32,3072]{1,0:T(8,128)(2,1)} %up_in.1) | copy-start | bytes 589828
  8.4 0.7 %copy-start.6 = (f32[1,1,2,2,256]{4,3,2,1,0:T(2,128)S(1)}, f32[1,1,2,2,256]{4,3,2,1,0:T(2,128)}, u32[]{:S(2)}) copy-start(f32[1,1,2,2,256]{4,3,2,1,0:T(2,128)} %param.15) | copy-start | bytes 12292
  9.1 0.7 %copy-start.7 = (s32[2,3]{1,0:T(2,128)S(1)}, s32[2,3]{1,0:T(2,128)}, u32[]{:S(2)}) copy-start(s32[2,3]{1,0:T(2,128)} %reach.1) | copy-start | bytes 76

commit v2 on v1

--- a/solution.py
+++ b/solution.py
@@ -32,8 +32,8 @@
     w_in,
     down_in,
     up_in,
-    reach,
-    valid,
+    reach_in,
+    valid_in,
     gq,
     gk,
     gv,
@@ -63,14 +63,14 @@
     dvb,
     mx_own,
     mx,
-    px_send,
-    px,
-    mine,
-    red,
-    rsb,
-    agb,
-    fin,
-    fx,
+    pa,
+    pb,
+    ra,
+    rb,
+    zb,
+    fq,
+    reach,
+    valid,
     lsem,
     q_send,
     q_recv,
@@ -84,12 +84,12 @@
     r_recv,
     mx_ssem,
     mx_rsem,
-    px_sem,
-    rs_ssem,
-    rs_rsem,
-    ag_ssem,
-    ag_rsem,
-    fx_sem,
+    oc_ssem,
+    oc_rsem,
+    z_ssem,
+    z_rsem,
+    f_ssem,
+    f_rsem,
     out_send,
     out_recv,
     out_sem,
@@ -101,9 +101,21 @@
     other = 1 - h
     left = lax.rem(t + t_size - 1, t_size)
     right = lax.rem(t + 1, t_size)
+    z_size = t_size // 2
+    y_size = g_size // 2
+    x_lo = t // z_size
+    z = lax.rem(t, z_size)
+    y = g // 2
+    x_hi = lax.rem(g, 2)
+    quarter = 2 * x_lo + h
     scale = hd**-0.5
     mine_lanes = pl.ds(pl.multiple_of(h * hd, hd), hd)
     other_lanes = pl.ds(pl.multiple_of(other * hd, hd), hd)
+
+    def quad(step):
+        peer = lax.rem(quarter + step, 4)
+        return peer, {"tm": lax.rem(peer // 2, 2) * z_size + z, "space": lax.rem(peer, 2)}
+
     sides = (right, left)
     partner = {"space": other}
 
@@ -127,6 +139,8 @@
         local(q_in.at[:, mine_lanes], qb.at[h], 5),
         local(k_in.at[:, mine_lanes], kb.at[h], 6),
         local(v_in.at[:, mine_lanes], vb.at[h], 7),
+        local(reach_in, reach, 10),
+        local(valid_in, valid, 11),
     ]
     for copy in loads[:4]:
         copy.start()
@@ -135,17 +149,14 @@
         copy.start()
 
     barrier = pltpu.get_barrier_semaphore()
-    for step in range(1, t_size):
-        pl.semaphore_signal(
-            barrier, inc=1, device_id={"tm": lax.rem(t + step, t_size)}, device_id_type=MESH
-        )
-    for step in range(1, g_size):
-        pl.semaphore_signal(
-            barrier, inc=1, device_id={"tensor": lax.rem(g + step, g_size)}, device_id_type=MESH
-        )
-    for where in (partner, {"tm": left, "space": other}, {"tm": right, "space": other}):
+    greeted = [{"tm": side, "space": n} for side in (left, right) for n in range(2)]
+    greeted += [{"tensor": lax.rem(y + step, y_size) * 2 + x_hi} for step in range(1, y_size)]
+    greeted += [quad(step)[1] for step in range(1, 4)]
+    greeted += [{**quad(step)[1], "tensor": 2 * y + 1 - x_hi} for step in range(4)]
+    greeted += [{"tm": x_lo * z_size + lax.rem(z + step, z_size)} for step in range(1, z_size)]
+    for where in greeted:
         pl.semaphore_signal(barrier, inc=1, device_id=where, device_id_type=MESH)
-    pl.semaphore_wait(barrier, t_size + g_size + 1)
+    pl.semaphore_wait(barrier, len(greeted))
 
     sends = []
     for side in range(2):
@@ -168,17 +179,17 @@
 
     loads[0].wait()
     loads[1].wait()
-    mixed_part = dot(down_v[...], o_v[...], (((0,), (1,)), ((), ())))
+    mixed_part = dot(down_v[...], o_v[...], NT)
     mx_own[...] = mixed_part.astype(bf16)
     mx_sends = []
-    for step in range(1, g_size):
+    for step in range(1, y_size):
         mx_sends.append(
             remote(
                 mx_own,
                 mx.at[step - 1],
                 mx_ssem.at[step - 1],
                 mx_rsem.at[step - 1],
-                {"tensor": lax.rem(g + step, g_size)},
+                {"tensor": lax.rem(y + step, y_size) * 2 + x_hi},
             )
         )
     for copy in mx_sends:
@@ -224,7 +235,7 @@
         cot = cot_v[rows, :]
         down_grad = (adapter_factor * dot(cot, up_v[...], NT)).astype(bf16)
         dmix[rows, :] = down_grad
-        grad = (dot(cot, w_v[...], NT) + dot(down_grad, down_v[...], NT)).astype(bf16)
+        grad = (dot(cot, w_v[...], NT) + dot(down_grad, down_v[...])).astype(bf16)
         product = (grad.astype(f32) * o_v[rows, :].astype(f32)).T
         for n in range(2):
             delta = jnp.sum(product[n * hd : (n + 1) * hd, :], axis=0, keepdims=True)
@@ -239,24 +250,101 @@
 
     lax.fori_loop(0, 2, project, 0)
 
-    for copy in mx_sends:
-        copy.wait_recv()
-    mixed = mx_own[...].astype(f32)
-    for step in range(1, g_size):
-        mixed += mx[step - 1].astype(f32)
-    columns = pl.ds(pl.multiple_of(g * cols, 128), cols)
-    up_part = dot(mixed.astype(bf16), cot_v[:, columns]) * (adapter_factor / total_tokens)
-    a_part = dot(dmix[...], o_v[...], TN) * (1.0 / total_tokens)
-    width = mine.shape[1]
-    if width > a_part.shape[1]:
-        a_part = jnp.concatenate(
-            [a_part, jnp.zeros((a_part.shape[0], width - a_part.shape[1]), f32)], axis=1
-        )
-    first = h == 0
-    mine[...] = jnp.where(first, up_part, a_part)
-    px_send[...] = jnp.where(first, a_part, up_part)
-    px_copy = remote(px_send, px, px_sem.at[0], px_sem.at[1], partner)
-    px_copy.start()
+    ranks = pa.shape[1]
+    features = ga.shape[1]
+    oct_sends = []
+    for step in range(4):
+        peer, where = quad(step)
+        if step:
+            oct_sends.append(
+                remote(
+                    pa.at[peer], ra.at[step - 1], oc_ssem.at[step - 1], oc_rsem.at[step - 1], where
+                )
+            )
+        oct_sends.append(
+            remote(
+                pb.at[peer],
+                rb.at[step],
+                oc_ssem.at[3 + step],
+                oc_rsem.at[3 + step],
+                {**where, "tensor": 2 * y + 1 - x_hi},
+            )
+        )
+    z_sends = []
+    for step in range(1, z_size):
+        z_sends.append(
+            remote(
+                zb.at[z],
+                zb.at[z],
+                z_ssem.at[step - 1],
+                z_rsem.at[step - 1],
+                {"tm": x_lo * z_size + lax.rem(z + step, z_size)},
+            )
+        )
+    quad_sends = []
+    for step in range(1, 4):
+        quad_sends.append(
+            remote(
+                fq.at[quarter], fq.at[quarter], f_ssem.at[step - 1], f_rsem.at[step - 1], quad(step)[1]
+            )
+        )
+
+    def adapter_parts():
+        for copy in mx_sends:
+            copy.wait_recv()
+        mixed = mx_own[...].astype(f32)
+        for index in range(y_size - 1):
+            mixed += mx[index].astype(f32)
+        mixed = mixed.astype(bf16)
+        parts = []
+        for side in range(2):
+            columns = pl.ds(pl.multiple_of((2 * y + side) * cols, 128), cols)
+            parts.append(dot(mixed, cot_v[:, columns]) * (adapter_factor / total_tokens))
+        a_part = dot(dmix[...], o_v[...], TN) * (1.0 / total_tokens)
+        first = x_hi == 0
+        same = jnp.where(first, parts[0], parts[1])
+        across = jnp.where(first, parts[1], parts[0])
+        for p in range(4):
+            rows = slice(p * ranks, (p + 1) * ranks)
+            pa[p, :, :cols] = same[rows, :]
+            pa[p, :, cols:] = a_part[rows, :]
+            pb[p] = across[rows, :]
+        for copy in oct_sends:
+            copy.start()
+
+    def adapter_z():
+        for copy in oct_sends:
+            copy.wait_recv()
+        total = pa[quarter]
+        for index in range(3):
+            total += ra[index]
+        up_total = total[:, :cols]
+        for index in range(4):
+            up_total += rb[index]
+        zb[z, :ranks, :cols] = up_total.astype(bf16)
+        zb[z, ranks:, :features] = total[:, cols:].astype(bf16)
+        for copy in z_sends:
+            copy.start()
+
+    def adapter_quad():
+        for copy in z_sends:
+            copy.wait_recv()
+        total = zb[0].astype(f32)
+        for index in range(1, z_size):
+            total += zb[index].astype(f32)
+        fq[quarter] = total
+        for copy in quad_sends:
+            copy.start()
+
+    def adapter_out():
+        for copy in quad_sends:
+            copy.wait_recv()
+        for p in range(4):
+            rows = slice(p * ranks, (p + 1) * ranks)
+            um[rows, :] = fq[p, :ranks, :cols]
+            ga[rows, :] = fq[p, ranks:, :features]
+
+    zb[z] = jnp.zeros(zb.shape[1:], bf16)
 
     for copy in loads[5:]:
         copy.wait()
@@ -271,112 +359,77 @@
     reach_h = reach[h, 1]
     reach_w = reach[h, 2]
 
-    share = red.shape[1]
-
-    def reduce_sends():
-        copies = []
-        for step in range(1, t_size):
-            peer = lax.rem(t + step, t_size)
-            copies.append(
-                remote(
-                    red.at[peer],
-                    rsb.at[step - 1],
-                    rs_ssem.at[step - 1],
-                    rs_rsem.at[step - 1],
-                    {"tm": peer},
-                )
-            )
-        return copies
-
-    def gather_sends():
-        copies = []
-        for step in range(1, t_size):
-            copies.append(
-                remote(
-                    agb.at[t],
-                    agb.at[t],
-                    ag_ssem.at[step - 1],
-                    ag_rsem.at[step - 1],
-                    {"tm": lax.rem(t + step, t_size)},
-                )
-            )
-        return copies
-
     def locate(u):
-        v = u - 4
-        near = u < 4
-        hq = jnp.where(near, lax.rem(h + u // 2, 2), lax.rem(v // 2 + 2, 2))
-        w = jnp.where(near, lax.rem(u, 2), v // 4)
-        f = jnp.where(near, 0, 1 + lax.rem(v + 4, 2))
-        return near, hq, w, f
-
-    def back(u):
-        _, hq, w, f = locate(u)
+        v = u - 2
+        near = u < 2
+        w = jnp.where(near, u, v // 2)
+        f = jnp.where(near, 0, 1 + lax.rem(v + 2, 2))
+        return near, w, f
+
+    def back(u, hq):
+        _, w, f = locate(u)
         rows = rows_of(w)
         where = {"tm": jnp.where(f == 1, left, right), "space": hq}
         slot = jnp.where(f == 1, 1, 0)
         return remote(
-            rq.at[u], ret.at[slot, h, rows], r_send.at[u], r_recv.at[slot * 2 + h, w], where
+            rq.at[u, hq], ret.at[slot, h, rows], r_send.at[u, hq], r_recv.at[slot * 2 + h, w], where
         )
 
     def back_pair(u):
-        _, hq, w, f = locate(u)
+        rows = rows_of(u)
         return remote(
-            rq.at[u], ret.at[2, h, rows_of(w)], r_send.at[u], r_recv.at[4 + h, w], partner
-        )
+            rq.at[u, other], ret.at[2, h, rows], r_send.at[u, other], r_recv.at[4 + h, u], partner
+        )
+
+    def arrive(slot, w):
+        rows = rows_of(w)
+        remote(st.at[slot, w], st.at[slot, w], s_send.at[0, 0], s_recv.at[slot, w], partner).wait_recv()
+        remote(
+            db.at[slot, rows], db.at[slot, rows], d_send.at[0, 0], d_recv.at[slot, w], partner
+        ).wait_recv()
+
+        @pl.when(w == 0)
+        def _():
+            remote(qb.at[slot], qb.at[slot], q_send.at[0], q_recv.at[slot], partner).wait_recv()
 
     def step(u, carry):
-        near, hq, w, f = locate(u)
-        slot = f * 2 + hq
+        near, w, f = locate(u)
         rows = rows_of(w)
+
+        @pl.when(near)
+        def _():
+            arrive(other, w)
+
+        @pl.when(u == 1)
+        def _():
+            adapter_parts()
+
+        @pl.when(u == 3)
+        def _():
+            adapter_z()
 
         @pl.when(u >= 2)
         def _():
-            remote(st.at[slot, w], st.at[slot, w], s_send.at[0, 0], s_recv.at[slot, w], partner).wait_recv()
-            remote(
-                db.at[slot, rows], db.at[slot, rows], d_send.at[0, 0], d_recv.at[slot, w], partner
-            ).wait_recv()
-
-        @pl.when((u >= 2) & (w == 0))
-        def _():
-            remote(qb.at[slot], qb.at[slot], q_send.at[0], q_recv.at[slot], partner).wait_recv()
-
-        @pl.when(u == 4)
-        def _():
-            px_copy.wait_recv()
-            chip = mine[...] + px[...]
-            for p in range(t_size):
-                red[p] = chip[p * share : (p + 1) * share, :]
-            for copy in reduce_sends():
-                copy.start()
-
-        @pl.when(u == 8)
-        def _():
-            for copy in reduce_sends():
-                copy.wait_recv()
-            total = red[t]
-            for index in range(t_size - 1):
-                total += rsb[index]
-            agb[t] = total
-            for copy in gather_sends():
-                copy.start()
-
-        q = qb[slot, rows, :]
-        d = db[slot, rows, :]
-        lse = st[slot, w, 0:1, :]
-        delta = st[slot, w, 1:2, :]
+            for hq in range(2):
+                arrive(2 * f + hq, w)
+
+        q = jnp.concatenate([qb[2 * f, rows, :], qb[2 * f + 1, rows, :]], axis=0)
+        d = jnp.concatenate([db[2 * f, rows, :], db[2 * f + 1, rows, :]], axis=0)
+        lse = [st[2 * f + hq, w, 0:1, :] for hq in range(2)]
+        delta = jnp.concatenate([st[2 * f + hq, w, 1:2, :] for hq in range(2)], axis=1)
         frame = t + jnp.where(f == 0, 0, jnp.where(f == 1, -1, 1))
         frame_ok = (frame >= 0) & (frame < t_size) & (jnp.where(f == 0, 0, 1) <= reach_t)
         dq = None
         for kt in range(4):
             hk, wk = kt // 2, kt % 2
-            linked = (
-                frame_ok
-                & (jnp.abs(hq - hk) <= reach_h)
-                & (jnp.abs(w - wk) <= reach_w)
-                & (valid[t, hk, wk] == 1)
-            )
-            shift = lse + jnp.where(linked, 0.0, FAR)
+            key_ok = frame_ok & (jnp.abs(w - wk) <= reach_w) & (valid[hk, wk, t] == 1)
+            shift = jnp.concatenate(
+                [
+                    lse[hq] + jnp.where(key_ok & (abs(hq - hk) <= reach_h), 0.0, FAR)
+                    for hq in range(2)
+                ],
+                axis=1,
+            )
             k = kb[hk, wk * tile : (wk + 1) * tile, :]
             v = vb[hk, wk * tile : (wk + 1) * tile, :]
             probs = jnp.exp2(dot(k, q, NT) * (scale * LOG2E) - shift)
@@ -387,23 +440,23 @@
             dk_acc[span, :] += dot(dscore, q)
             part = dot(kt_buf[:, span], dscore)
             dq = part if dq is None else dq + part
-        rq[u] = (dq * scale).T.astype(bf16)
-
-        @pl.when(u >= 4)
+        dq_rows = (dq * scale).T.astype(bf16)
+        for hq in range(2):
+            rq[u, hq] = dq_rows[hq * tile : (hq + 1) * tile, :]
+
+        @pl.when(u >= 2)
         def _():
-            back(u).start()
-
-        @pl.when((u >= 2) & (u < 4))
+            for hq in range(2):
+                back(u, hq).start()
+
+        @pl.when(near)
         def _():
             back_pair(u).start()
-
-        @pl.when(u < 2)
-        def _():
-            ret[2, h, rows, :] = rq[u]
+            ret[2, h, rows, :] = rq[u, h]
 
         return carry
 
-    lax.fori_loop(0, 12, step, 0)
+    lax.fori_loop(0, 6, step, 0)
 
     for row in range(2):
         dkb[row] = (dk_acc[row * 2 * tile : (row + 1) * 2 * tile, :] * scale).astype(bf16)
@@ -419,13 +472,7 @@
     for copy in pair_out + own_out:
         copy.start()
 
-    gathers = gather_sends()
-    for copy in gathers:
-        copy.wait_recv()
-    for p in range(t_size):
-        fin[p * share : (p + 1) * share, :] = agb[p]
-    fx_copy = remote(fin, fx, fx_sem.at[0], fx_sem.at[1], partner)
-    fx_copy.start()
+    adapter_quad()
 
     for w in range(2):
         rows = rows_of(w)
@@ -450,27 +497,32 @@
     gq_copy = pltpu.make_async_copy(gq_v, gq, out_sem.at[2])
     gq_copy.start()
 
-    fx_copy.wait_recv()
-    um[...] = jnp.where(first, fin[...], fx[...])[:, :cols]
-    ga[...] = jnp.where(first, fx[...], fin[...])[:, : ga.shape[0]].T
-
-    for copy in sends + mx_sends + [px_copy, fx_copy] + pair_out + gathers + reduce_sends():
+    adapter_out()
+
+    for copy in sends + mx_sends + oct_sends + z_sends + quad_sends + pair_out:
         copy.wait_send()
     for w in range(2):
         for copy in grad_sends(w):
             copy.wait_send()
 
     def drain(u, carry):
-        back(u).wait_send()
+        for hq in range(2):
+            back(u, hq).wait_send()
         return carry
 
-    lax.fori_loop(4, 12, drain, 0)
-    for u in (2, 3):
+    lax.fori_loop(2, 6, drain, 0)
+    for u in range(2):
         back_pair(u).wait_send()
     for copy in pair_out:
         copy.wait_recv()
     for copy in own_out + [gq_copy]:
         copy.wait()
+
+
+def finish(*refs):
+    count = len(refs) // 2
+    for index in range(count):
+        refs[count + index][...] = refs[index][...]
 
 
 def body(
@@ -498,13 +550,15 @@
     total_tokens = t_size * lax.axis_size("space") * tokens
     cols = model // g_size
     width = max(cols, features)
-    share = rank // t_size
+    ranks = rank // 4
+    y_size = g_size // 2
     sizes = (tile, hd, t_size, g_size, total_tokens, cols)
 
     def flat(array):
         return array.reshape(tokens, array.shape[-1])
 
     anywhere = pl.BlockSpec(memory_space=pl.ANY)
+    hbm = pl.BlockSpec(memory_space=pltpu.HBM)
     vmem = pl.BlockSpec(memory_space=pltpu.VMEM)
     smem = pl.BlockSpec(memory_space=pltpu.SMEM)
     dma = pltpu.SemaphoreType.DMA
@@ -520,29 +574,29 @@
         pltpu.VMEM((2, heads, tile), f32),
         pltpu.VMEM((tokens, model), bf16),
         pltpu.VMEM((features, model), bf16),
-        pltpu.VMEM((features, rank), bf16),
+        pltpu.VMEM((rank, features), bf16),
         pltpu.VMEM((rank, model), bf16),
         pltpu.VMEM((2, tokens, hd), bf16),
         pltpu.VMEM((2, 2, 8, tile), f32),
         pltpu.VMEM((tokens, rank), bf16),
         pltpu.VMEM((2 * tokens, hd), f32),
         pltpu.VMEM((2 * tokens, hd), f32),
-        pltpu.VMEM((12, tile, hd), bf16),
+        pltpu.VMEM((6, 2, tile, hd), bf16),
         pltpu.VMEM((3, 2, tokens, hd), bf16),
         pltpu.VMEM((tokens, features), bf16),
         pltpu.VMEM((2, tokens, hd), bf16),
         pltpu.VMEM((2, tokens, hd), bf16),
         pltpu.VMEM((rank, tokens), bf16),
-        pltpu.VMEM((g_size - 1, rank, tokens), bf16),
-        pltpu.VMEM((rank, width), f32),
-        pltpu.VMEM((rank, width), f32),
-        pltpu.VMEM((rank, width), f32),
-        pltpu.VMEM((t_size, share, width), f32),
-        pltpu.VMEM((t_size - 1, share, width), f32),
-        pltpu.VMEM((t_size, share, width), f32),
-        pltpu.VMEM((rank, width), f32),
-        pltpu.VMEM((rank, width), f32),
-        dma((10,)),
+        pltpu.VMEM((max(y_size - 1, 1), rank, tokens), bf16),
+        pltpu.VMEM((4, ranks, cols + features), f32),
+        pltpu.VMEM((4, ranks, cols), f32),
+        pltpu.VMEM((3, ranks, cols + features), f32),
+        pltpu.VMEM((4, ranks, cols), f32),
+        pltpu.VMEM((t_size // 2, 2 * ranks, width), bf16),
+        pltpu.VMEM((4, 2 * ranks, width), f32),
+        pltpu.SMEM(head_tile_reach.shape, jnp.int32),
+        pltpu.SMEM(key_tile_valid.shape[1:] + key_tile_valid.shape[:1], jnp.int32),
+        dma((12,)),
         dma((5,)),
         dma((6,)),
         dma((2, 5)),
@@ -551,34 +605,34 @@
         dma((6, 2)),
         dma((2,)),
         dma((2,)),
-        dma((12,)),
         dma((6, 2)),
-        dma((g_size - 1,)),
-        dma((g_size - 1,)),
-        dma((2,)),
-        dma((t_size - 1,)),
-        dma((t_size - 1,)),
-        dma((t_size - 1,)),
-        dma((t_size - 1,)),
-        dma((2,)),
+        dma((6, 2)),
+        dma((max(y_size - 1, 1),)),
+        dma((max(y_size - 1, 1),)),
+        dma((7,)),
+        dma((7,)),
+        dma((t_size // 2 - 1,)),
+        dma((t_size // 2 - 1,)),
+        dma((3,)),
+        dma((3,)),
         dma((2,)),
         dma((2,)),
         dma((3,)),
     ]
-    grad_q, grad_k, grad_v, grad_a, up_map_gradient = pl.pallas_call(
+    results = pl.pallas_call(
         functools.partial(kernel, sizes),
         out_shape=(
             grads,
             grads,
             grads,
-            jax.ShapeDtypeStruct((features, rank), f32),
+            jax.ShapeDtypeStruct((rank, features), f32),
             jax.ShapeDtypeStruct((rank, cols), f32),
         ),
-        in_specs=[anywhere] * 9 + [smem] * 2,
+        in_specs=[hbm] * 11,
         out_specs=(anywhere, anywhere, anywhere, vmem, vmem),
         scratch_shapes=scratch,
         compiler_params=pltpu.CompilerParams(
-            collective_id=0, has_side_effects=True, vmem_limit_bytes=48 * 1024 * 1024
+            collective_id=0, has_side_effects=True, vmem_limit_bytes=62 * 1024 * 1024
         ),
     )(
         flat(queries),
@@ -588,16 +642,23 @@
         row_logsumexp.reshape(row_logsumexp.shape[2:]),
         flat(output_cotangent),
         output_weight,
-        adapter_down,
+        adapter_down.T,
         adapter_up,
         head_tile_reach,
-        key_tile_valid,
+        jnp.transpose(key_tile_valid, (1, 2, 0)),
     )
+    grad_q, grad_k, grad_v, grad_a, up_map_gradient = pl.pallas_call(
+        finish,
+        out_shape=tuple(jax.ShapeDtypeStruct(array.shape, array.dtype) for array in results),
+        in_specs=[vmem] * 5,
+        out_specs=(vmem,) * 5,
+        compiler_params=pltpu.CompilerParams(vmem_limit_bytes=62 * 1024 * 1024),
+    )(*results)
     return (
         grad_q.reshape(queries.shape),
         grad_k.reshape(queries.shape),
         grad_v.reshape(queries.shape),
-        grad_a,
+        grad_a.T,
         up_map_gradient,
     )
 

time: 63.6 us -> 43 us (0.68)
  the two profiles are of different devices: /device:TPU:1 before, /device:TPU:15 now
where the time goes in v2:
time: 43 us; the launch traced here: 42.4 us
  Pallas kernels  41.8 us (97%)
  between operations  0.64 us (1%)
    pallas_call x1, Pallas kernels, body(): pl.pallas_call(functools.partial(kernel, sizes), out_shape=(grads, grads,...  39.7 us
    pallas_call x1, Pallas kernels, body(): pl.pallas_call(finish, out_shape=tuple((jax.ShapeDtypeStruct(array.shape,...  2.04 us

profile of v2, /device:TPU:15, one launch (start us, length us, event | category | flops | bytes accessed | tf_op | source)
XLA Modules:
  0.0 42.4 jit_solution(6517356693750025077)
XLA Ops:
  0.6 39.7 %shard_map.146 = (bf16[512,256]{1,0:T(8,128)(2,1)}, bf16[512,256]{1,0:T(8,128)(2,1)}, bf16[512,256]{1,0:T(8,128)(2,1)}, f32[32,256]{1,0:T(8,128)}, f32[32,384]{1,0:T(8,128)}) custom-call(bf16[512,256]{1,0:T(8,128)(2,1)} %bitcast.13, bf16[512,256]{1,0:T(8,128)(2,1)} %bitcast.14, bf16[512,256]{1,0:T(8,128)(2,1)} %bitcast.15, bf16[512,256]{1,0:T(8,128)(2,1)} %bitcast.16, ...), custom_call_target="tpu_custom_call" | custom-call | tf_op jit(solution)/shard_map/pallas_call | solution.py:622
  40.4 2.0 %shard_map.147 = (bf16[512,256]{1,0:T(8,128)(2,1)}, bf16[512,256]{1,0:T(8,128)(2,1)}, bf16[512,256]{1,0:T(8,128)(2,1)}, f32[32,256]{1,0:T(8,128)}, f32[32,384]{1,0:T(8,128)}) custom-call(bf16[512,256]{1,0:T(8,128)(2,1)} %get-tuple-element.15.refs_0_, bf16[512,256]{1,0:T(8,128)(2,1)} %get-tuple-element.16.refs_1_, ...), custom_call_target="tpu_custom_call" | custom-call | tf_op jit(solution)/shard_map/pallas_call | solution.py:650

commit v3 on v2

--- a/solution.py
+++ b/solution.py
@@ -118,6 +118,7 @@
 
     sides = (right, left)
     partner = {"space": other}
+    has = (t < t_size - 1, t > 0)
 
     def local(src, dst, index):
         return pltpu.make_async_copy(src, dst, lsem.at[index])
@@ -156,31 +157,13 @@
     greeted += [{"tm": x_lo * z_size + lax.rem(z + step, z_size)} for step in range(1, z_size)]
     for where in greeted:
         pl.semaphore_signal(barrier, inc=1, device_id=where, device_id_type=MESH)
-    pl.semaphore_wait(barrier, len(greeted))
-
-    sends = []
-    for side in range(2):
-        for n in range(2):
-            sends.append(
-                remote(
-                    q_in.at[:, n * hd : (n + 1) * hd],
-                    qb.at[2 + 2 * side + h],
-                    q_send.at[side * 2 + n],
-                    q_recv.at[2 + 2 * side + h],
-                    {"tm": sides[side], "space": n},
-                )
-            )
-    q_pair = remote(q_in.at[:, other_lanes], qb.at[h], q_send.at[4], q_recv.at[h], partner)
-    k_pair = remote(k_in.at[:, other_lanes], kb.at[h], kv_send.at[0], kv_recv.at[0], partner)
-    v_pair = remote(v_in.at[:, other_lanes], vb.at[h], kv_send.at[1], kv_recv.at[1], partner)
-    sends += [q_pair, k_pair, v_pair]
-    for copy in sends:
-        copy.start()
-
     loads[0].wait()
     loads[1].wait()
     mixed_part = dot(down_v[...], o_v[...], NT)
     mx_own[...] = mixed_part.astype(bf16)
+
+    pl.semaphore_wait(barrier, len(greeted))
+
     mx_sends = []
     for step in range(1, y_size):
         mx_sends.append(
@@ -195,32 +178,56 @@
     for copy in mx_sends:
         copy.start()
 
+    def q_sends(side):
+        return [
+            remote(
+                q_in.at[:, n * hd : (n + 1) * hd],
+                qb.at[2 + 2 * side + h],
+                q_send.at[side * 2 + n],
+                q_recv.at[2 + 2 * side + h],
+                {"tm": sides[side], "space": n},
+            )
+            for n in range(2)
+        ]
+
+    q_pair = remote(q_in.at[:, other_lanes], qb.at[h], q_send.at[4], q_recv.at[h], partner)
+    k_pair = remote(k_in.at[:, other_lanes], kb.at[h], kv_send.at[0], kv_recv.at[0], partner)
+    v_pair = remote(v_in.at[:, other_lanes], vb.at[h], kv_send.at[1], kv_recv.at[1], partner)
+    sends = [q_pair, k_pair, v_pair]
+    for copy in sends:
+        copy.start()
+    for side in range(2):
+
+        @pl.when(has[side])
+        def _():
+            for copy in q_sends(side):
+                copy.start()
+
+
     loads[2].wait()
     loads[3].wait()
     loads[4].wait()
 
-    def grad_sends(w):
+    def grad_far(w, side):
         copies = []
         rows = rows_of(w)
-        for side in range(2):
-            for n in range(2):
-                slot = 2 + 2 * side + h
-                where = {"tm": sides[side], "space": n}
-                index = side * 2 + n
-                copies.append(
-                    remote(
-                        stsend.at[n, w], st.at[slot, w], s_send.at[w, index], s_recv.at[slot, w], where
-                    )
+        for n in range(2):
+            slot = 2 + 2 * side + h
+            where = {"tm": sides[side], "space": n}
+            index = side * 2 + n
+            copies.append(
+                remote(stsend.at[n, w], st.at[slot, w], s_send.at[w, index], s_recv.at[slot, w], where)
+            )
+            copies.append(
+                remote(
+                    dsend.at[n, rows], db.at[slot, rows], d_send.at[w, index], d_recv.at[slot, w], where
                 )
-                copies.append(
-                    remote(
-                        dsend.at[n, rows],
-                        db.at[slot, rows],
-                        d_send.at[w, index],
-                        d_recv.at[slot, w],
-                        where,
-                    )
-                )
+            )
+        return copies
+
+    def grad_pair(w):
+        copies = []
+        rows = rows_of(w)
         copies.append(
             remote(stsend.at[other, w], st.at[h, w], s_send.at[w, 4], s_recv.at[h, w], partner)
         )
@@ -244,13 +251,12 @@
             dsend[n, rows, :] = grad[:, n * hd : (n + 1) * hd]
         db[h, rows, :] = dsend[h, rows, :]
         st[h, w] = stsend[h, w]
-        for copy in grad_sends(w):
-            copy.start()
         return carry
 
     lax.fori_loop(0, 2, project, 0)
 
-    ranks = pa.shape[1]
+    ranks = pa.shape[1] // 2
+    lanes = pb.shape[2]
     features = ga.shape[1]
     oct_sends = []
     for step in range(4):
@@ -306,23 +312,27 @@
         across = jnp.where(first, parts[1], parts[0])
         for p in range(4):
             rows = slice(p * ranks, (p + 1) * ranks)
-            pa[p, :, :cols] = same[rows, :]
-            pa[p, :, cols:] = a_part[rows, :]
-            pb[p] = across[rows, :]
+            pa[p, :ranks, :cols] = same[rows, :].astype(bf16)
+            pa[p, ranks:, :features] = a_part[rows, :].astype(bf16)
+            pb[p, :ranks, :] = across[rows, :lanes].astype(bf16)
+            pb[p, ranks:, : cols - lanes] = across[rows, lanes:].astype(bf16)
         for copy in oct_sends:
             copy.start()
 
     def adapter_z():
         for copy in oct_sends:
             copy.wait_recv()
-        total = pa[quarter]
+        total = pa[quarter].astype(f32)
         for index in range(3):
-            total += ra[index]
-        up_total = total[:, :cols]
-        for index in range(4):
-            up_total += rb[index]
+            total += ra[index].astype(f32)
+        other_up = rb[0].astype(f32)
+        for index in range(1, 4):
+            other_up += rb[index].astype(f32)
+        up_total = total[:ranks, :cols] + jnp.concatenate(
+            [other_up[:ranks, :], other_up[ranks:, : cols - lanes]], axis=1
+        )
         zb[z, :ranks, :cols] = up_total.astype(bf16)
-        zb[z, ranks:, :features] = total[:, cols:].astype(bf16)
+        zb[z, ranks:, :features] = total[ranks:, :features].astype(bf16)
         for copy in z_sends:
             copy.start()
 
@@ -345,6 +355,22 @@
             ga[rows, :] = fq[p, ranks:, :features]
 
     zb[z] = jnp.zeros(zb.shape[1:], bf16)
+    pa[...] = jnp.zeros_like(pa)
+    pb[...] = jnp.zeros_like(pb)
+
+    def start_far(w):
+        for side in range(2):
+
+            @pl.when(has[side])
+            def _():
+                for copy in grad_far(w, side):
+                    copy.start()
+
+    for copy in grad_pair(0) + grad_pair(1):
+        copy.start()
+    start_far(0)
+    adapter_parts()
+    start_far(1)
 
     for copy in loads[5:]:
         copy.wait()
@@ -355,6 +381,16 @@
     for row in range(2):
         kt_buf[:, row * 2 * tile : (row + 1) * 2 * tile] = kb[row].T
 
+    for side in range(2):
+
+        @pl.when(jnp.logical_not(has[1 - side]))
+        def _():
+            for slot in (2 + 2 * side, 3 + 2 * side):
+                qb[slot] = jnp.zeros(qb.shape[1:], bf16)
+                db[slot] = jnp.zeros(db.shape[1:], bf16)
+                st[slot] = jnp.zeros(st.shape[1:], f32)
+            ret[side] = jnp.zeros(ret.shape[1:], bf16)
+
     reach_t = reach[h, 0]
     reach_h = reach[h, 1]
     reach_w = reach[h, 2]
@@ -363,16 +399,19 @@
         v = u - 2
         near = u < 2
         w = jnp.where(near, u, v // 2)
-        f = jnp.where(near, 0, 1 + lax.rem(v + 2, 2))
-        return near, w, f
-
-    def back(u, hq):
-        _, w, f = locate(u)
-        rows = rows_of(w)
-        where = {"tm": jnp.where(f == 1, left, right), "space": hq}
-        slot = jnp.where(f == 1, 1, 0)
+        row = lax.rem(v + 2, 2)
+        slots = (jnp.where(near, 0, 2 + row), jnp.where(near, 1, 4 + row))
+        return near, w, row, slots
+
+    def back(u, side):
+        _, w, row, _ = locate(u)
+        where = {"tm": (left, right)[side], "space": row}
         return remote(
-            rq.at[u, hq], ret.at[slot, h, rows], r_send.at[u, hq], r_recv.at[slot * 2 + h, w], where
+            rq.at[u, side],
+            ret.at[1 - side, h, rows_of(w)],
+            r_send.at[u, side],
+            r_recv.at[2 * (1 - side) + h, w],
+            where,
         )
 
     def back_pair(u):
@@ -393,40 +432,42 @@
             remote(qb.at[slot], qb.at[slot], q_send.at[0], q_recv.at[slot], partner).wait_recv()
 
     def step(u, carry):
-        near, w, f = locate(u)
+        near, w, row, slots = locate(u)
         rows = rows_of(w)
 
         @pl.when(near)
         def _():
             arrive(other, w)
 
-        @pl.when(u == 1)
-        def _():
-            adapter_parts()
-
-        @pl.when(u == 3)
+        @pl.when(u == 4)
         def _():
             adapter_z()
 
         @pl.when(u >= 2)
         def _():
-            for hq in range(2):
-                arrive(2 * f + hq, w)
-
-        q = jnp.concatenate([qb[2 * f, rows, :], qb[2 * f + 1, rows, :]], axis=0)
-        d = jnp.concatenate([db[2 * f, rows, :], db[2 * f + 1, rows, :]], axis=0)
-        lse = [st[2 * f + hq, w, 0:1, :] for hq in range(2)]
-        delta = jnp.concatenate([st[2 * f + hq, w, 1:2, :] for hq in range(2)], axis=1)
-        frame = t + jnp.where(f == 0, 0, jnp.where(f == 1, -1, 1))
-        frame_ok = (frame >= 0) & (frame < t_size) & (jnp.where(f == 0, 0, 1) <= reach_t)
+            for side in range(2):
+
+                @pl.when(has[1 - side])
+                def _():
+                    arrive(slots[side], w)
+
+        q = jnp.concatenate([qb[slot, rows, :] for slot in slots], axis=0)
+        d = jnp.concatenate([db[slot, rows, :] for slot in slots], axis=0)
+        lse = [st[slot, w, 0:1, :] for slot in slots]
+        delta = jnp.concatenate([st[slot, w, 1:2, :] for slot in slots], axis=1)
+        frame_ok = [near | ((reach_t >= 1) & (t > 0)), near | ((reach_t >= 1) & (t < t_size - 1))]
+        height = [jnp.where(near, 0, row), jnp.where(near, 1, row)]
         dq = None
         for kt in range(4):
             hk, wk = kt // 2, kt % 2
-            key_ok = frame_ok & (jnp.abs(w - wk) <= reach_w) & (valid[hk, wk, t] == 1)
+            key_ok = (jnp.abs(w - wk) <= reach_w) & (valid[hk, wk, t] == 1)
             shift = jnp.concatenate(
                 [
-                    lse[hq] + jnp.where(key_ok & (abs(hq - hk) <= reach_h), 0.0, FAR)
-                    for hq in range(2)
+                    lse[side]
+                    + jnp.where(
+                        key_ok & frame_ok[side] & (jnp.abs(height[side] - hk) <= reach_h), 0.0, FAR
+                    )
+                    for side in range(2)
                 ],
                 axis=1,
             )
@@ -441,13 +482,14 @@
             part = dot(kt_buf[:, span], dscore)
             dq = part if dq is None else dq + part
         dq_rows = (dq * scale).T.astype(bf16)
-        for hq in range(2):
-            rq[u, hq] = dq_rows[hq * tile : (hq + 1) * tile, :]
-
-        @pl.when(u >= 2)
-        def _():
-            for hq in range(2):
-                back(u, hq).start()
+        for side in range(2):
+            rq[u, side] = dq_rows[side * tile : (side + 1) * tile, :]
+
+        for side in range(2):
+
+            @pl.when((u >= 2) & has[1 - side])
+            def _():
+                back(u, side).start()
 
         @pl.when(near)
         def _():
@@ -476,16 +518,21 @@
 
     for w in range(2):
         rows = rows_of(w)
-        for slot in range(4):
-            remote(
-                ret.at[slot // 2, slot % 2, rows],
-                ret.at[slot // 2, slot % 2, rows],
-                r_send.at[0],
-                r_recv.at[slot, w],
-                partner,
-            ).wait_recv()
+        for side in range(2):
+
+            @pl.when(has[1 - side])
+            def _():
+                for n in range(2):
+                    remote(
+                        ret.at[side, n, rows],
+                        ret.at[side, n, rows],
+                        r_send.at[0, 0],
+                        r_recv.at[2 * side + n, w],
+                        partner,
+                    ).wait_recv()
+
         remote(
-            ret.at[2, other, rows], ret.at[2, other, rows], r_send.at[0], r_recv.at[4 + other, w], partner
+            ret.at[2, other, rows], ret.at[2, other, rows], r_send.at[0, 0], r_recv.at[4 + other, w], partner
         ).wait_recv()
         for n in range(2):
             total = (
@@ -502,12 +549,26 @@
     for copy in sends + mx_sends + oct_sends + z_sends + quad_sends + pair_out:
         copy.wait_send()
     for w in range(2):
-        for copy in grad_sends(w):
+        for copy in grad_pair(w):
             copy.wait_send()
+    for side in range(2):
+
+        @pl.when(has[side])
+        def _():
+            for copy in q_sends(side):
+                copy.wait_send()
+            for w in range(2):
+                for copy in grad_far(w, side):
+                    copy.wait_send()
+
 
     def drain(u, carry):
-        for hq in range(2):
-            back(u, hq).wait_send()
+        for side in range(2):
+
+            @pl.when(has[1 - side])
+            def _():
+                back(u, side).wait_send()
+
         return carry
 
     lax.fori_loop(2, 6, drain, 0)
@@ -551,6 +612,7 @@
     cols = model // g_size
     width = max(cols, features)
     ranks = rank // 4
+    lanes = -(-cols // 256) * 128
     y_size = g_size // 2
     sizes = (tile, hd, t_size, g_size, total_tokens, cols)
 
@@ -588,10 +650,10 @@
         pltpu.VMEM((2, tokens, hd), bf16),
         pltpu.VMEM((rank, tokens), bf16),
         pltpu.VMEM((max(y_size - 1, 1), rank, tokens), bf16),
-        pltpu.VMEM((4, ranks, cols + features), f32),
-        pltpu.VMEM((4, ranks, cols), f32),
-        pltpu.VMEM((3, ranks, cols + features), f32),
-        pltpu.VMEM((4, ranks, cols), f32),
+        pltpu.VMEM((4, 2 * ranks, width), bf16),
+        pltpu.VMEM((4, 2 * ranks, lanes), bf16),
+        pltpu.VMEM((3, 2 * ranks, width), bf16),
+        pltpu.VMEM((4, 2 * ranks, lanes), bf16),
         pltpu.VMEM((t_size // 2, 2 * ranks, width), bf16),
         pltpu.VMEM((4, 2 * ranks, width), f32),
         pltpu.SMEM(head_tile_reach.shape, jnp.int32),

time: 43 us -> 38.1 us (0.89); the launches traced: 42.4 us -> 38 us
  Pallas kernels: 41.8 us -> 37.3 us
    pallas_call x1, Pallas kernels: 39.7 us -> 35.3 us  [body(): pl.pallas_call(functools.partial(kernel, sizes), out_shape=(grads, grads,...]
where the time goes in v3:
time: 38.1 us; the launch traced here: 38 us
  Pallas kernels  37.3 us (98%)
  between operations  0.64 us (2%)
    pallas_call x1, Pallas kernels, body(): pl.pallas_call(functools.partial(kernel, sizes), out_shape=(grads, grads,...  35.3 us
    pallas_call x1, Pallas kernels, body(): pl.pallas_call(finish, out_shape=tuple((jax.ShapeDtypeStruct(array.shape,...  2.04 us

profile of v3, /device:TPU:15, one launch (start us, length us, event | category | flops | bytes accessed | tf_op | source)
XLA Modules:
  0.0 38.0 jit_solution(11272021483699312548)
XLA Ops:
  0.6 35.3 %shard_map.146 = (bf16[512,256]{1,0:T(8,128)(2,1)}, bf16[512,256]{1,0:T(8,128)(2,1)}, bf16[512,256]{1,0:T(8,128)(2,1)}, f32[32,256]{1,0:T(8,128)}, f32[32,384]{1,0:T(8,128)}) custom-call(bf16[512,256]{1,0:T(8,128)(2,1)} %bitcast.13, bf16[512,256]{1,0:T(8,128)(2,1)} %bitcast.14, bf16[512,256]{1,0:T(8,128)(2,1)} %bitcast.15, bf16[512,256]{1,0:T(8,128)(2,1)} %bitcast.16, ...), custom_call_target="tpu_custom_call" | custom-call | tf_op jit(solution)/shard_map/pallas_call | solution.py:684
  35.9 2.0 %shard_map.147 = (bf16[512,256]{1,0:T(8,128)(2,1)}, bf16[512,256]{1,0:T(8,128)(2,1)}, bf16[512,256]{1,0:T(8,128)(2,1)}, f32[32,256]{1,0:T(8,128)}, f32[32,384]{1,0:T(8,128)}) custom-call(bf16[512,256]{1,0:T(8,128)(2,1)} %get-tuple-element.15.refs_0_, bf16[512,256]{1,0:T(8,128)(2,1)} %get-tuple-element.16.refs_1_, ...), custom_call_target="tpu_custom_call" | custom-call | tf_op jit(solution)/shard_map/pallas_call | solution.py:712

commit v4 on v3

--- a/solution.py
+++ b/solution.py
@@ -37,8 +37,7 @@
     gq,
     gk,
     gv,
-    ga,
-    um,
+    fq,
     qb,
     db,
     st,
@@ -68,7 +67,7 @@
     ra,
     rb,
     zb,
-    fq,
+    f_own,
     reach,
     valid,
     lsem,
@@ -257,7 +256,7 @@
 
     ranks = pa.shape[1] // 2
     lanes = pb.shape[2]
-    features = ga.shape[1]
+    features = o_v.shape[1]
     oct_sends = []
     for step in range(4):
         peer, where = quad(step)
@@ -291,9 +290,11 @@
     for step in range(1, 4):
         quad_sends.append(
             remote(
-                fq.at[quarter], fq.at[quarter], f_ssem.at[step - 1], f_rsem.at[step - 1], quad(step)[1]
-            )
-        )
+                f_own, fq.at[quarter], f_ssem.at[step - 1], f_rsem.at[step - 1], quad(step)[1]
+            )
+        )
+
+    f_copy = pltpu.make_async_copy(f_own, fq.at[quarter], out_sem.at[3])
 
     def adapter_parts():
         for copy in mx_sends:
@@ -342,17 +343,9 @@
         total = zb[0].astype(f32)
         for index in range(1, z_size):
             total += zb[index].astype(f32)
-        fq[quarter] = total
-        for copy in quad_sends:
+        f_own[...] = total.astype(bf16)
+        for copy in quad_sends + [f_copy]:
             copy.start()
-
-    def adapter_out():
-        for copy in quad_sends:
-            copy.wait_recv()
-        for p in range(4):
-            rows = slice(p * ranks, (p + 1) * ranks)
-            um[rows, :] = fq[p, :ranks, :cols]
-            ga[rows, :] = fq[p, ranks:, :features]
 
     zb[z] = jnp.zeros(zb.shape[1:], bf16)
     pa[...] = jnp.zeros_like(pa)
@@ -544,7 +537,8 @@
     gq_copy = pltpu.make_async_copy(gq_v, gq, out_sem.at[2])
     gq_copy.start()
 
-    adapter_out()
+    for copy in quad_sends:
+        copy.wait_recv()
 
     for copy in sends + mx_sends + oct_sends + z_sends + quad_sends + pair_out:
         copy.wait_send()
@@ -576,14 +570,30 @@
         back_pair(u).wait_send()
     for copy in pair_out:
         copy.wait_recv()
-    for copy in own_out + [gq_copy]:
+    for copy in own_out + [gq_copy, f_copy]:
         copy.wait()
 
 
-def finish(*refs):
-    count = len(refs) // 2
-    for index in range(count):
-        refs[count + index][...] = refs[index][...]
+def finish(gq_in, gk_in, gv_in, fq_in, gq, gk, gv, ga, um, gq_v, gk_v, gv_v, fq_v, ga_v, um_v, sems):
+    pairs = ((fq_in, fq_v), (gq_in, gq_v), (gk_in, gk_v), (gv_in, gv_v))
+    reads = [pltpu.make_async_copy(*pair, sems.at[0, i]) for i, pair in enumerate(pairs)]
+    pairs = ((ga_v, ga), (gq_v, gq), (gk_v, gk), (gv_v, gv), (um_v, um))
+    writes = [pltpu.make_async_copy(*pair, sems.at[1, i]) for i, pair in enumerate(pairs)]
+    for copy in reads:
+        copy.start()
+    for i in range(1, 4):
+        reads[i].wait()
+        writes[i].start()
+    reads[0].wait()
+    ranks = fq_v.shape[1] // 2
+    for p in range(4):
+        rows = slice(p * ranks, (p + 1) * ranks)
+        um_v[rows, :] = fq_v[p, :ranks, : um_v.shape[1]].astype(f32)
+        ga_v[rows, :] = fq_v[p, ranks:, : ga_v.shape[1]].astype(f32)
+    writes[0].start()
+    writes[4].start()
+    for copy in writes:
+        copy.wait()
 
 
 def body(
@@ -621,8 +631,6 @@
 
     anywhere = pl.BlockSpec(memory_space=pl.ANY)
     hbm = pl.BlockSpec(memory_space=pltpu.HBM)
-    vmem = pl.BlockSpec(memory_space=pltpu.VMEM)
-    smem = pl.BlockSpec(memory_space=pltpu.SMEM)
     dma = pltpu.SemaphoreType.DMA
     grads = jax.ShapeDtypeStruct((tokens, features), bf16)
     scratch = [
@@ -655,7 +663,7 @@
         pltpu.VMEM((3, 2 * ranks, width), bf16),
         pltpu.VMEM((4, 2 * ranks, lanes), bf16),
         pltpu.VMEM((t_size // 2, 2 * ranks, width), bf16),
-        pltpu.VMEM((4, 2 * ranks, width), f32),
+        pltpu.VMEM((2 * ranks, width), bf16),
         pltpu.SMEM(head_tile_reach.shape, jnp.int32),
         pltpu.SMEM(key_tile_valid.shape[1:] + key_tile_valid.shape[:1], jnp.int32),
         dma((12,)),
@@ -679,7 +687,7 @@
         dma((3,)),
         dma((2,)),
         dma((2,)),
-        dma((3,)),
+        dma((4,)),
     ]
     results = pl.pallas_call(
         functools.partial(kernel, sizes),
@@ -687,11 +695,10 @@
             grads,
             grads,
             grads,
-            jax.ShapeDtypeStruct((rank, features), f32),
-            jax.ShapeDtypeStruct((rank, cols), f32),
+            jax.ShapeDtypeStruct((4, 2 * ranks, width), bf16),
         ),
         in_specs=[hbm] * 11,
-        out_specs=(anywhere, anywhere, anywhere, vmem, vmem),
+        out_specs=(anywhere,) * 4,
         scratch_shapes=scratch,
         compiler_params=pltpu.CompilerParams(
             collective_id=0, has_side_effects=True, vmem_limit_bytes=62 * 1024 * 1024
@@ -709,11 +716,14 @@
         head_tile_reach,
         jnp.transpose(key_tile_valid, (1, 2, 0)),
     )
+    totals = (jax.ShapeDtypeStruct((rank, features), f32), jax.ShapeDtypeStruct((rank, cols), f32))
     grad_q, grad_k, grad_v, grad_a, up_map_gradient = pl.pallas_call(
         finish,
-        out_shape=tuple(jax.ShapeDtypeStruct(array.shape, array.dtype) for array in results),
-        in_specs=[vmem] * 5,
-        out_specs=(vmem,) * 5,
+        out_shape=(grads, grads, grads, *totals),
+        in_specs=[anywhere] * 4,
+        out_specs=(anywhere,) * 5,
+        scratch_shapes=[pltpu.VMEM(array.shape, array.dtype) for array in (*results, *totals)]
+        + [dma((2, 5))],
         compiler_params=pltpu.CompilerParams(vmem_limit_bytes=62 * 1024 * 1024),
     )(*results)
     return (

time: 38.1 us -> 37.3 us (0.979)
  Pallas kernels: 37.3 us -> 36.3 us
    pallas_call x1, Pallas kernels: 35.3 us -> 34.4 us  [body(): pl.pallas_call(functools.partial(kernel, sizes), out_shape=(grads, grads,...]
where the time goes in v4:
time: 37.3 us; the launch traced here: 37 us
  Pallas kernels  36.3 us (97%)
  between operations  0.64 us (2%)
    pallas_call x1, Pallas kernels, body(): pl.pallas_call(functools.partial(kernel, sizes), out_shape=(grads, grads,...  34.4 us
    pallas_call x1, Pallas kernels, body(): pl.pallas_call(finish, out_shape=(grads, grads, grads, *totals), in_specs...  1.96 us

profile of v4, /device:TPU:15, one launch (start us, length us, event | category | flops | bytes accessed | tf_op | source)
XLA Modules:
  0.0 37.0 jit_solution(4347720415673792829)
XLA Ops:
  0.6 34.4 %shard_map.146 = (bf16[512,256]{1,0:T(8,128)(2,1)}, bf16[512,256]{1,0:T(8,128)(2,1)}, bf16[512,256]{1,0:T(8,128)(2,1)}, bf16[4,16,384]{2,1,0:T(8,128)(2,1)}) custom-call(bf16[512,256]{1,0:T(8,128)(2,1)} %bitcast.13, bf16[512,256]{1,0:T(8,128)(2,1)} %bitcast.14, bf16[512,256]{1,0:T(8,128)(2,1)} %bitcast.15, bf16[512,256]{1,0:T(8,128)(2,1)} %bitcast.16, ...), custom_call_target="tpu_custom_call" | custom-call | tf_op jit(solution)/shard_map/pallas_call | solution.py:692
  35.0 2.0 %shard_map.147 = (bf16[512,256]{1,0:T(8,128)(2,1)}, bf16[512,256]{1,0:T(8,128)(2,1)}, bf16[512,256]{1,0:T(8,128)(2,1)}, f32[32,256]{1,0:T(8,128)}, f32[32,384]{1,0:T(8,128)}) custom-call(bf16[512,256]{1,0:T(8,128)(2,1)} %get-tuple-element.14.gq_in, bf16[512,256]{1,0:T(8,128)(2,1)} %get-tuple-element.15.gk_in, bf16[512,256]{1,0:T(8,128)(2,1)} %get-tuple-element.16.gv_in, ...), custom_call_target="tpu_custom_call" | custom-call | tf_op jit(solution)/shard_map/pallas_call | solution.py:720

commit v5 on v4

--- a/solution.py
+++ b/solution.py
@@ -493,9 +493,11 @@
 
     lax.fori_loop(0, 6, step, 0)
 
-    for row in range(2):
-        dkb[row] = (dk_acc[row * 2 * tile : (row + 1) * 2 * tile, :] * scale).astype(bf16)
-        dvb[row] = dv_acc[row * 2 * tile : (row + 1) * 2 * tile, :].astype(bf16)
+    def convert(row):
+        rows = pl.ds(pl.multiple_of(row * 2 * tile, 2 * tile), 2 * tile)
+        dkb[row] = (dk_acc[rows, :] * scale).astype(bf16)
+        dvb[row] = dv_acc[rows, :].astype(bf16)
+
     pair_out = [
         remote(dkb.at[other], gk.at[:, mine_lanes], out_send.at[0], out_recv.at[0], partner),
         remote(dvb.at[other], gv.at[:, mine_lanes], out_send.at[1], out_recv.at[1], partner),
@@ -504,11 +506,19 @@
         pltpu.make_async_copy(dkb.at[h], gk.at[:, mine_lanes], out_sem.at[0]),
         pltpu.make_async_copy(dvb.at[h], gv.at[:, mine_lanes], out_sem.at[1]),
     ]
-    for copy in pair_out + own_out:
+    convert(other)
+    for copy in pair_out:
         copy.start()
+    convert(h)
+    for copy in own_out:
+        copy.start()
 
     adapter_quad()
 
+    gq_copies = [
+        pltpu.make_async_copy(gq_v.at[rows_of(w)], gq.at[rows_of(w)], out_sem.at[2 + 2 * w])
+        for w in range(2)
+    ]
     for w in range(2):
         rows = rows_of(w)
         for side in range(2):
@@ -534,8 +544,7 @@
                 + ret[2, n, rows, :].astype(f32)
             )
             gq_v[rows, n * hd : (n + 1) * hd] = total.astype(bf16)
-    gq_copy = pltpu.make_async_copy(gq_v, gq, out_sem.at[2])
-    gq_copy.start()
+        gq_copies[w].start()
 
     for copy in quad_sends:
         copy.wait_recv()
@@ -570,7 +579,7 @@
         back_pair(u).wait_send()
     for copy in pair_out:
         copy.wait_recv()
-    for copy in own_out + [gq_copy, f_copy]:
+    for copy in own_out + gq_copies + [f_copy]:
         copy.wait()
 
 
@@ -687,7 +696,7 @@
         dma((3,)),
         dma((2,)),
         dma((2,)),
-        dma((4,)),
+        dma((5,)),
     ]
     results = pl.pallas_call(
         functools.partial(kernel, sizes),

time: 37.3 us -> 37.3 us (level)
  no operation moved by 1% of the time
where the time goes in v5:
time: 37.3 us; the launch traced here: 37 us
  Pallas kernels  36.3 us (97%)
  between operations  0.64 us (2%)
    pallas_call x1, Pallas kernels, body(): pl.pallas_call(functools.partial(kernel, sizes), out_shape=(grads, grads,...  34.4 us
    pallas_call x1, Pallas kernels, body(): pl.pallas_call(finish, out_shape=(grads, grads, grads, *totals), in_specs...  1.96 us

profile of v5, /device:TPU:15, one launch (start us, length us, event | category | flops | bytes accessed | tf_op | source)
XLA Modules:
  0.0 37.0 jit_solution(17277638422874444040)
XLA Ops:
  0.6 34.4 %shard_map.146 = (bf16[512,256]{1,0:T(8,128)(2,1)}, bf16[512,256]{1,0:T(8,128)(2,1)}, bf16[512,256]{1,0:T(8,128)(2,1)}, bf16[4,16,384]{2,1,0:T(8,128)(2,1)}) custom-call(bf16[512,256]{1,0:T(8,128)(2,1)} %bitcast.13, bf16[512,256]{1,0:T(8,128)(2,1)} %bitcast.14, bf16[512,256]{1,0:T(8,128)(2,1)} %bitcast.15, bf16[512,256]{1,0:T(8,128)(2,1)} %bitcast.16, ...), custom_call_target="tpu_custom_call" | custom-call | tf_op jit(solution)/shard_map/pallas_call | solution.py:701
  35.0 2.0 %shard_map.147 = (bf16[512,256]{1,0:T(8,128)(2,1)}, bf16[512,256]{1,0:T(8,128)(2,1)}, bf16[512,256]{1,0:T(8,128)(2,1)}, f32[32,256]{1,0:T(8,128)}, f32[32,384]{1,0:T(8,128)}) custom-call(bf16[512,256]{1,0:T(8,128)(2,1)} %get-tuple-element.14.gq_in, bf16[512,256]{1,0:T(8,128)(2,1)} %get-tuple-element.15.gk_in, bf16[512,256]{1,0:T(8,128)(2,1)} %get-tuple-element.16.gv_in, ...), custom_call_target="tpu_custom_call" | custom-call | tf_op jit(solution)/shard_map/pallas_call | solution.py:729
